TPU v7x, 32 devices: a whole 2x2x4 slice. The times are simulated.
32 devices in a mesh: pole: 2 (over core), row: 4 (over y, x), col: 4 (over z).
Axes of the slice: x: 2, y: 2, z: 4, core: 2. Of those that a mesh axis runs over, the one named last changes fastest.
Arguments:
- inverse_block: bfloat16 [2, 2, 4, 4, 256, 4096], P('pole', None, None, 'row', None, 'col'), may hold values from -5 to 5
- panels: bfloat16 [2, 3, 2, 4, 4, 256, 256], P('pole', None, None, 'col', 'row'), may hold values from -0.09375 to 0.09375
- panel_mask: int32 [3, 4, 4], P(None, 'col', 'row'), may hold values 0 or 1
- parent_panels: float32 [2, 2, 2, 256, 256], P('pole'), may hold values from -0.25 to 0.25
- diag_inverse: float32 [2, 3, 2, 256, 256], P('pole'), may hold values from -6 to 6
- pole_weights: float32 [2, 2], P('pole'), may hold values from 0.5 to 1.5
Outputs:
- density_panel: float32 [3, 4, 4, 256, 256], P(None, 'col', 'row', None, 'pole')
- density_diag: float32 [3, 256, 256], replicated
Inputs may be any that keep to these rules, and one draw needn't show every extreme that they name: panel_mask[k, a, b] is 1 where the block of 256 ancestor rows (a, b) of supernode k's factor panel may be nonzero, 0 where it is structurally zero.
All inputs are finite; a program needn't handle non-finite values.
Results may differ from a plain program's by a relative error of at most 0.0003.
Values may be sent and summed in bfloat16 or wider, within the bound.
No kernel may reach another device: no remote copies, remote signals or barrier semaphores. Data moves between devices by JAX's collectives and lax.ppermute only.
A program may use at most 64 MiB of HBM per device.

v0:
```python
import functools

import jax
import jax.numpy as jnp
from jax import lax
from jax.experimental import pallas as pl
from jax.experimental.pallas import tpu as pltpu
from jax.sharding import PartitionSpec as P

F32 = jnp.float32
BF16 = jnp.bfloat16
WHOLE = pl.BlockSpec(memory_space=pltpu.VMEM)
SCALARS = pl.BlockSpec(memory_space=pltpu.SMEM)
ANYWHERE = pl.BlockSpec(memory_space=pl.ANY)
FAR = pl.BlockSpec(memory_space=pltpu.HBM)


def params(mebibytes):
    return pltpu.CompilerParams(vmem_limit_bytes=mebibytes << 20)


def small_cost():
    return pl.CostEstimate(flops=1, bytes_accessed=1, transcendentals=0)


def large_cost():
    return pl.CostEstimate(flops=10**11, bytes_accessed=1, transcendentals=0)


def mm(left, right):
    return jnp.dot(left, right, preferred_element_type=F32)


def mm_t(left, right):
    return lax.dot_general(left, right, (((1,), (1,)), ((), ())), preferred_element_type=F32)


def split(value):
    high = value.astype(BF16)
    return high, (value - high.astype(F32)).astype(BF16)


def exchange(value, axes, count, distance):
    return lax.ppermute(value, axes, [(i, i ^ distance) for i in range(count)])


def tree_sum(values):
    while len(values) > 1:
        values = [values[i] + values[i + 1] for i in range(0, len(values), 2)]
    return values[0]


def xor_order(stack, me, count):
    bits = count.bit_length() - 1
    rest = stack.shape[1:]
    values = stack.reshape((2,) * bits + rest)
    for axis in range(bits):
        bit = (me >> (bits - 1 - axis)) & 1
        values = jnp.where(bit == 1, jnp.flip(values, axis), values)
    return values.reshape((count,) + rest)


def mask_kernel(levels, keep, flag_ref, panel_ref, *refs):
    refs = list(refs)
    if keep:
        refs.pop(0)
    out_refs = [refs.pop(0) for _ in levels]
    kept_refs = [refs.pop(0) for _ in range(2)] if keep else None
    buf, flags, sems = refs
    first = 0 if keep else levels[0]
    copies = [
        pltpu.make_async_copy(panel_ref.at[pl.ds(first, buf.shape[0])], buf, sems.at[0]),
        pltpu.make_async_copy(flag_ref, flags, sems.at[1]),
    ]
    for copy in copies:
        copy.start()
    for copy in copies:
        copy.wait()
    for k in range(buf.shape[0]):
        flag = flags[first + k].astype(F32)
        for part in range(2):
            value = buf[k, part].astype(F32) * flag
            if keep:
                kept_refs[part][k] = value.astype(BF16)
            if first + k in levels:
                out_refs[levels.index(first + k)][part] = value.T.astype(BF16)


def parent_kernel(parent_ref, out_ref):
    for k in range(parent_ref.shape[0]):
        real_high, real_low = split(parent_ref[k, 0].T)
        imag_high, imag_low = split(parent_ref[k, 1].T)
        high = left_block(real_high, imag_high)
        wide = high.shape[1]
        out_ref[k, :, :wide] = high
        out_ref[k, :, wide : 2 * wide] = high
        out_ref[k, :, 2 * wide :] = left_block(real_low, imag_low)


def left_block(real, imag):
    return jnp.concatenate(
        [jnp.concatenate([real, -imag], axis=1), jnp.concatenate([imag, real], axis=1)], axis=0
    )


class Slots:
    def __init__(self, slots):
        self.operands = []
        self.slots = []
        for slot in slots:
            self.slots.append([(self.place(array), index) for array, index in slot])

    def place(self, array):
        for n, operand in enumerate(self.operands):
            if operand is array:
                return n
        self.operands.append(array)
        return len(self.operands) - 1

    def left(self, refs, n, inner):
        parts = []
        for part in range(2):
            values = [
                refs[at][part] if index is None else refs[at][index, part]
                for at, index in self.slots[n]
            ]
            parts.append(values[0] if len(values) == 1 else jnp.where(inner == 1, *values))
        return left_block(*parts)


def block_copies(block_ref, buf, sem, owners, my_row, rows, height, ordered):
    copies = []
    for n, owner in enumerate(owners):
        if not ordered:
            copies.append([pltpu.make_async_copy(block_ref.at[:, owner], buf.at[n], sem.at[n, 0])])
            continue
        copies.append(
            [
                pltpu.make_async_copy(
                    block_ref.at[
                        :, owner, :, pl.ds(pl.multiple_of((my_row ^ t) * height, height), height)
                    ],
                    buf.at[n, :, :, pl.ds(t * height, height)],
                    sem.at[n, t],
                )
                for t in range(rows)
            ]
        )
    return copies


def early_products(rows, width, height, ordered, place, level_slots, late, blocks, after):
    levels = len(level_slots)
    count = len(level_slots[0])
    slots = Slots([slot for level in level_slots for slot in level])
    local = rows * height

    def kernel(place_ref, block_ref, *refs):
        piece_refs = refs[: len(slots.operands)]
        out_refs = refs[len(slots.operands) + len(after) :][:levels]
        late_ref, buf, left_buf, sem, late_sem = refs[-5:]
        my_row = place_ref[1]
        owners = [place_ref[4 + n] for n in range(count)]
        copies = block_copies(block_ref, buf, sem, owners, my_row, rows, height, ordered)
        owners = [place_ref[4 + count + n] for n in range(late)]
        late_copies = sum(
            block_copies(block_ref, late_ref, late_sem, owners, my_row, rows, height, ordered), []
        )
        for copy in sum(copies, []) + late_copies:
            copy.start()
        for level in range(levels):
            for n in range(count):
                left_buf[
                    level * 2 * width : (level + 1) * 2 * width,
                    n * 2 * height : (n + 1) * 2 * height,
                ] = slots.left(piece_refs, level * count + n, place_ref[0])
        for copy in sum(copies, []):
            copy.wait()
        right = buf[...].reshape(count * 2 * height, local)
        for level in range(levels):
            left = left_buf[level * 2 * width : (level + 1) * 2 * width, :]
            out_refs[level][...] = mm(left, right)
        for copy in late_copies:
            copy.wait()

    outs = [jax.ShapeDtypeStruct((2 * width, local), F32)] * levels
    outs.append(jax.ShapeDtypeStruct((late, 2, height, local), BF16))
    return pl.pallas_call(
        kernel,
        out_shape=outs,
        in_specs=[SCALARS, FAR] + [WHOLE] * len(slots.operands) + [ANYWHERE] * len(after),
        out_specs=[WHOLE] * len(outs),
        scratch_shapes=[
            pltpu.VMEM((count, 2, height, local), BF16),
            pltpu.VMEM((levels * 2 * width, count * 2 * height), BF16),
            pltpu.SemaphoreType.DMA((count, rows)),
            pltpu.SemaphoreType.DMA((late, rows)),
        ],
        compiler_params=params(24),
        cost_estimate=large_cost(),
        name="early",
    )(place, blocks, *slots.operands, *after)


def pack_panels(levels, rows, width, height, packed, reals, imags):
    chunks = rows if packed else 1
    chunk = height if packed else rows * height
    slots = Slots([reals, imags])

    def kernel(*refs):
        panel_refs = refs[: len(slots.operands)]
        out_ref, sem = refs[len(slots.operands) :]
        copies = []
        for p in range(2):
            for r in range(rows):
                at, index = slots.slots[p][r]
                source = panel_refs[at] if index is None else panel_refs[at].at[index]
                target = out_ref.at[
                    :, r if packed else 0,
                    pl.ds(0 if packed else r * height, height),
                    pl.ds(p * width, width),
                ]
                copies.append(pltpu.make_async_copy(source, target, sem.at[r, p]))
        for copy in copies:
            copy.start()
        for copy in copies:
            copy.wait()

    return pl.pallas_call(
        kernel,
        out_shape=jax.ShapeDtypeStruct((levels, chunks, chunk, 2 * width), BF16),
        in_specs=[ANYWHERE] * len(slots.operands),
        out_specs=WHOLE,
        scratch_shapes=[pltpu.SemaphoreType.DMA((rows, 2))],
        compiler_params=params(8),
        cost_estimate=large_cost(),
        name="pack_rows",
    )(*slots.operands)


def level_products(
    rows, width, height, packed, level, place, weights, level_slots, blocks, panels,
    total, rest, next_total, parents, next_diag, after,
):
    count = len(level_slots)
    slots = Slots(level_slots)
    has_next = next_total is not None
    local = rows * height
    half = width // 2
    part = half // rows
    wide = 2 * width
    kinds = 2 if has_next else 1

    def kernel(*refs):
        refs = list(refs)

        def take(n):
            return [refs.pop(0) for _ in range(n)]

        place_ref, weight_ref = take(2)
        piece_refs = take(len(slots.operands))
        block_ref, panel_ref, total_ref, rest_ref = take(4)
        if has_next:
            next_total_ref, parent_ref, next_diag_ref = take(3)
        take(len(after))
        if has_next:
            next_out_ref, next_rest_ref = take(2)
        out_refs = take(3) if packed else take(2)
        left_buf, x_buf, sums, diag_buf = take(4)
        assert not refs

        inner, my_row, pole = place_ref[0], place_ref[1], place_ref[2]
        first = place_ref[3].astype(F32)
        weight_real = weight_ref[0]
        weight_imag = weight_ref[1]

        for n in range(count):
            left_buf[:, n * 2 * height : (n + 1) * 2 * height] = slots.left(piece_refs, n, inner)

        late = mm(left_buf[...], block_ref[...].reshape(count * 2 * height, local))
        x = -(total_ref[...] + late)
        term = weight_real * x[width:] + weight_imag * x[:width]
        if packed:
            low, upper = term[:half], term[half:]
            mine = jnp.where(pole == 0, low, upper)
            sent = jnp.where(pole == 0, upper, low)
            for t in range(rows):
                columns = slice(t * height, (t + 1) * height)
                out_refs[0][t, :half, :] = mine[:, columns]
                out_refs[1 + 2 * t // rows][t % (rows // 2), :half, :] = sent[:, columns]
        else:
            out_refs[0][...] = term
        x_high, x_low = split(x)
        x_buf[:wide] = x_high
        x_buf[wide : 2 * wide] = x_low
        if has_next:
            x_buf[2 * wide :] = x_high
        for k in range(kinds):
            both = mm(x_buf[: 2 * wide], panel_ref[level + k].reshape(local, wide))
            sums[:, k * wide : (k + 1) * wide] = both[:wide] + both[wide:]
        if has_next:
            next_out_ref[...] = next_total_ref[...] + mm(parent_ref[level], x_buf[...])

        def complex_sum(k):
            at = k * wide
            real = sums[:width, at : at + width] - sums[width:, at + width : at + wide]
            imag = sums[:width, at + width : at + wide] + sums[width:, at : at + width]
            return real, imag

        own_real, own_imag = complex_sum(0)
        scale = first if level == 0 else 1.0
        y_real = rest_ref[0] * scale - own_real.T
        y_imag = rest_ref[1] * scale - own_imag.T
        diag_buf[...] = weight_real * y_imag + weight_imag * y_real
        if packed:
            for t in range(rows):
                places = ((out_refs[0], t, pole), (out_refs[1 + 2 * t // rows], t % (rows // 2), 1 - pole))
                for ref, n, side in places:
                    at = pl.multiple_of(side * half + (my_row ^ t) * part, part)
                    ref[n, half:, :] = diag_buf[pl.ds(at, part), :]
        else:
            out_refs[1][...] = diag_buf[...]
        if has_next:
            parent = parent_ref[level]
            parent_high, parent_low = parent[:, :wide], parent[:, 2 * wide :]
            follow_real, follow_imag = complex_sum(1)
            y_high, y_low = split(jnp.concatenate([y_real, y_imag], axis=1))
            mixed = mm_t(y_high, parent_high) + mm_t(y_low, parent_high) + mm_t(y_high, parent_low)
            z = -jnp.concatenate(
                [follow_real + mixed[:, :width], follow_imag + mixed[:, width:]], axis=0
            )
            z_high, z_low = split(z)
            back = mm(parent, jnp.concatenate([z_high, z_low, z_high], axis=0))
            next_rest_ref[0] = next_diag_ref[0] * first - back[:width]
            next_rest_ref[1] = next_diag_ref[1] * first - back[width:]

    operands = [place, weights] + slots.operands + [blocks, panels, total, rest]
    specs = [SCALARS, SCALARS] + [WHOLE] * (len(slots.operands) + 4)
    outs = []
    aliases = {}
    if has_next:
        aliases = {len(operands): 0}
        operands += [next_total, parents, next_diag]
        specs += [WHOLE] * 3
        outs += [
            jax.ShapeDtypeStruct((wide, local), F32),
            jax.ShapeDtypeStruct((2, width, width), F32),
        ]
    operands += after
    specs += [ANYWHERE] * len(after)
    if packed:
        outs.append(jax.ShapeDtypeStruct((rows, half + part, height), F32))
        outs += [jax.ShapeDtypeStruct((rows // 2, half + part, height), F32)] * 2
    else:
        outs += [
            jax.ShapeDtypeStruct((width, local), F32),
            jax.ShapeDtypeStruct((width, width), F32),
        ]
    return pl.pallas_call(
        kernel,
        out_shape=outs,
        in_specs=specs,
        out_specs=[WHOLE] * len(outs),
        input_output_aliases=aliases,
        scratch_shapes=[
            pltpu.VMEM((wide, count * 2 * height), BF16),
            pltpu.VMEM(((3 if has_next else 2) * wide, local), BF16),
            pltpu.VMEM((wide, kinds * wide), F32),
            pltpu.VMEM((width, width), F32),
        ],
        compiler_params=params(24),
        cost_estimate=large_cost(),
        name="level_%d" % level,
    )(*operands)


def join(values, after=()):
    def kernel(*refs):
        for n in range(len(values)):
            refs[-1][n] = refs[n][...]

    return pl.pallas_call(
        kernel,
        out_shape=jax.ShapeDtypeStruct((len(values),) + values[0].shape, values[0].dtype),
        in_specs=[WHOLE] * len(values) + [ANYWHERE] * len(after),
        out_specs=WHOLE,
        compiler_params=params(8),
        cost_estimate=small_cost(),
        name="join",
    )(*values, *after)


def cut(values, begin, after):
    count, height, width = len(values), values[0].shape[1] - begin, values[0].shape[2]

    def kernel(*refs):
        for n in range(count):
            refs[-1][n] = refs[n][0, begin:]

    return pl.pallas_call(
        kernel,
        out_shape=jax.ShapeDtypeStruct((count, height, width), F32),
        in_specs=[WHOLE] * count + [ANYWHERE] * len(after),
        out_specs=WHOLE,
        compiler_params=params(8),
        cost_estimate=small_cost(),
        name="cut",
    )(*values, *after)


def gate(values, after):
    count = len(values)

    def kernel(*refs):
        for n in range(count):
            refs[n - count][...] = refs[n][...]

    return pl.pallas_call(
        kernel,
        out_shape=[jax.ShapeDtypeStruct(value.shape, value.dtype) for value in values],
        in_specs=[WHOLE] * count + [ANYWHERE] * len(after),
        out_specs=[WHOLE] * count,
        compiler_params=params(8),
        cost_estimate=small_cost(),
        name="gate",
    )(*values, *after)


def add_parts(kept, received):
    levels = len(kept)
    rows = kept[0].shape[0]

    def kernel(*refs):
        for k in range(levels):
            for t in range(rows):
                got = refs[levels + 2 * k + 2 * t // rows][t % (rows // 2)]
                refs[3 * levels + t][k] = refs[k][t] + got

    return pl.pallas_call(
        kernel,
        out_shape=[jax.ShapeDtypeStruct((levels,) + kept[0].shape[1:], F32)] * rows,
        in_specs=[WHOLE] * (3 * levels),
        out_specs=[WHOLE] * rows,
        compiler_params=params(12),
        cost_estimate=small_cost(),
        name="add_parts",
    )(*kept, *received)


def gather_four(piece, me, axis, after, held, level):
    inner = (me == 1) | (me == 2)
    pairs = [(0, 1), (1, 0), (2, 3), (3, 2)]
    middle_pairs = [(1, 2), (2, 1)]
    outer_pairs = [(1, 0), (2, 3)]
    owners = [
        me,
        me ^ 1,
        jnp.where(inner, 3 - me, me ^ 2),
        jnp.where(inner, (3 - me) ^ 1, me ^ 3),
    ]
    near = lax.ppermute(piece, axis, pairs)
    joined = join([piece, near], after + held)
    middle = lax.ppermute(joined, axis, middle_pairs)
    if level == 0:
        outers = [(lax.ppermute(middle[n], axis, outer_pairs), None) for n in range(2)]
    else:
        outer = lax.ppermute(middle, axis, outer_pairs)
        outers = [(outer, n) for n in range(2)]
    far = [[(middle, n), outers[n]] for n in range(2)]
    after[:] = [joined]
    return owners, [[(piece, None)], [(near, None)]], far


def gather_line(piece, me, count, axis):
    owners, slots = [me], [[(piece, None)]]
    from_left = from_right = piece
    for step in range(1, count):
        from_left = lax.ppermute(from_left, axis, [(i, i + 1) for i in range(step - 1, count - 1)])
        from_right = lax.ppermute(from_right, axis, [(i, i - 1) for i in range(1, count - step + 1)])
        if 2 * step >= count:
            owners.append(jnp.clip(jnp.where(me >= step, me - step, me + step), 0, count - 1))
            slots.append([(jnp.where(me >= step, from_left, from_right), None)])
        else:
            owners += [jnp.maximum(me - step, 0), jnp.minimum(me + step, count - 1)]
            slots += [[(from_left, None)], [(from_right, None)]]
    return owners, slots[:1], slots[1:]


def gather_rows(value, near, far):
    first = exchange(value, "row", 4, near)
    joined = join([value, first])
    second = exchange(joined, "row", 4, far)
    found = {0: (value, None), near: (first, None), far: (second, 0), 3: (second, 1)}
    return [found[t] for t in range(4)], first, joined


def gather(piece, me, count, axis, after, held, level):
    if count == 4:
        return gather_four(piece, me, axis, after, held, level)
    return gather_line(piece, me, count, axis)


def make_per_device(sizes):
    poles, rows, cols = sizes

    def per_device(inverse_block, panels, panel_mask, parent_panels, diag_inverse, pole_weights):
        levels = panels.shape[1]
        height = panels.shape[5]
        width = panels.shape[6]
        half = width // 2
        part = half // rows
        packed = (
            poles == 2
            and rows & (rows - 1) == 0
            and cols & (cols - 1) == 0
            and height == width
            and height % 128 == 0
            and part % 8 == 0
        )
        my_pole = lax.axis_index("pole")
        my_row = lax.axis_index("row")
        my_col = lax.axis_index("col")
        first = ((my_row == 0) & (my_col == 0)).astype(jnp.int32)
        inner = ((my_col == 1) | (my_col == 2)).astype(jnp.int32)
        blocks = inverse_block[0, :, :, 0]
        local_panels = panels[0, :, :, 0, 0]
        flags = panel_mask[:, 0, 0]
        weights = pole_weights[0]
        flipped = (2, width, height)

        def masked(which, after):
            keep = bool(after)
            outs = [jax.ShapeDtypeStruct(flipped, BF16)] * len(which)
            if keep:
                outs += [jax.ShapeDtypeStruct((levels, height, width), BF16)] * 2
            return pl.pallas_call(
                functools.partial(mask_kernel, which, keep),
                out_shape=outs,
                in_specs=[FAR, FAR] + [ANYWHERE] * len(after),
                out_specs=[WHOLE] * len(outs),
                scratch_shapes=[
                    pltpu.VMEM((levels if keep else len(which),) + local_panels.shape[1:], BF16),
                    pltpu.SMEM((levels,), jnp.int32),
                    pltpu.SemaphoreType.DMA((2,)),
                ],
                compiler_params=params(8),
                cost_estimate=small_cost(),
                name="mask_rows" if keep else "mask",
            )(flags, local_panels, *after)

        pieces = list(masked([0], []))
        *more, kept_real, kept_imag = masked(list(range(1, levels)), pieces)
        pieces += more
        parents = pl.pallas_call(
            parent_kernel,
            out_shape=jax.ShapeDtypeStruct((levels - 1, 2 * width, 6 * width), BF16),
            in_specs=[WHOLE],
            out_specs=WHOLE,
            compiler_params=params(12),
            cost_estimate=small_cost(),
            name="parents",
        )(parent_panels[0])
        held = [[] for _ in pieces]
        if packed and rows == 4:
            reals, *steps_real = gather_rows(kept_real, 1, 2)
            imags, *steps_imag = gather_rows(kept_imag, 2, 1)
            held[1] = [steps_real[0], steps_imag[0]]
            held[2] = [steps_real[1], steps_imag[1]]
        elif packed:
            reals, imags = [
                [(value, None)]
                + [(exchange(value, "row", rows, t), None) for t in range(1, rows)]
                for value in (kept_real, kept_imag)
            ]
        else:
            reals, imags = [
                [(piece, None) for piece in lax.all_gather(value, "row")]
                for value in (kept_real, kept_imag)
            ]

        after = []
        gathered = []
        for k, piece in enumerate(pieces):
            gathered.append(gather(piece, my_col, cols, "col", after, held[k], k))

        def sum_rows(stack):
            return tree_sum([stack[0]] + [exchange(stack[t], "row", rows, t) for t in range(1, rows)])

        def spread(piece):
            whole = tree_sum([piece] + [exchange(piece, "col", cols, t) for t in range(1, cols)])
            whole = jnp.stack([whole] + [exchange(whole, "row", rows, t) for t in range(1, rows)])
            whole = xor_order(whole, my_row, rows)
            other = exchange(whole, "pole", 2, 1)
            return xor_order(jnp.stack([whole, other]), my_pole, 2)

        owners = gathered[0][0]
        place = jnp.stack(
            [jnp.asarray(v, jnp.int32) for v in [inner, my_row, my_pole, first] + owners]
        )
        late = len(gathered[0][2])
        *totals, late_blocks = early_products(
            rows,
            width,
            height,
            packed,
            place,
            [g[1] for g in gathered],
            late,
            blocks,
            [g[2][0][0][0] for g in gathered[:-1] if len(g[2][0]) == 2],
        )
        row_panels = pack_panels(levels, rows, width, height, packed, reals, imags)
        rest = diag_inverse[0, 0]
        panel_parts = []
        diag_parts = []
        kept = []
        received = []
        sums = []
        first_sum = []
        far_ordered = [s[1][0] for s in gathered[-1][2][:1] if len(s) == 2]
        ordered = [g[2][0][0][0] for g in gathered[1:-1] if len(g[2][0]) == 2]
        for level in range(levels):
            has_next = level + 1 < levels
            outs = level_products(
                rows,
                width,
                height,
                packed,
                level,
                place,
                weights,
                gathered[level][2],
                late_blocks,
                row_panels,
                totals[level],
                rest,
                totals[level + 1] if has_next else None,
                parents,
                diag_inverse[0, level + 1] if has_next else None,
                ordered if level == 0 else first_sum,
            )
            if has_next:
                totals[level + 1] = outs[0]
                rest = outs[1]
                outs = outs[2:]
            if packed:
                kept.append(outs[0])
                sent = outs[1:] if has_next else gate(outs[1:], sums)
                received += [exchange(value, "pole", 2, 1) for value in sent]
                parts = add_parts(kept, received)
                mine = sum_rows(parts)
                first_sum = [parts[0]]
                sums.append(mine)
                kept, received = [], []
            else:
                mine = lax.psum_scatter(outs[0], "row", scatter_dimension=1, tiled=True)
                mine = lax.psum_scatter(mine, "pole", scatter_dimension=0, tiled=True)
                panel_parts.append(mine.T)
                diag_parts.append(lax.psum(outs[1], ("pole", "row", "col")))
        if packed:
            panel_parts = [mine[0, :half].T for mine in sums]
            got = spread(cut(sums, half, []))
            diag_parts = [got[:, :, n].reshape(width, width) for n in range(levels)]
        return jnp.stack(panel_parts)[:, None, None], jnp.stack(diag_parts)

    return per_device


def solution(mesh):
    placed = (
        P("pole", None, None, "row", None, "col"),
        P("pole", None, None, "col", "row", None, None),
        P(None, "col", "row"),
        P("pole", None, None, None, None),
        P("pole", None, None, None, None),
        P("pole", None),
    )
    return jax.shard_map(
        make_per_device((mesh.shape["pole"], mesh.shape["row"], mesh.shape["col"])),
        mesh=mesh,
        in_specs=placed,
        out_specs=(P(None, "col", "row", None, "pole"), P()),
        check_vma=False,
    )
```

profile of v0, /device:TPU:0, one launch (start us, length us, event | category | flops | bytes accessed | tf_op | source)
XLA Modules:
  0.0 125.2 jit_solution(9359547272629266427)
XLA Ops:
  0.6 1.1 copy-done
  1.8 0.7 copy-done.16
  2.4 0.7 mask.1.refs_0_
  3.2 3.1 %collective-permute-start = (bf16[2,256,256]{2,1,0:T(8,128)(2,1)S(1)}, bf16[2,256,256]{2,1,0:T(8,128)(2,1)S(1)}, u32[]{:S(2)}, u32[]{:S(2)}) collective-permute-start(bf16[2,256,256]{2,1,0:T(8,128)(2,1)S(1)} %mask.1.refs_0_), channel_id=1, source_target_pairs={{0,1},{1,0},{2,3},{3,2},{4,5},{5,4},{6,7},{7,6},{8,9},{9,8},{10,11... | collective-permute-start | bytes 786440 | tf_op jit(solution)/shard_map/ppermute | solution.py:461
  6.2 1.5 %mask_rows.1 = (bf16[2,256,256]{2,1,0:T(8,128)(2,1)S(1)}, bf16[2,256,256]{2,1,0:T(8,128)(2,1)}, bf16[3,256,256]{2,1,0:T(8,128)(2,1)S(1)}, bf16[3,256,256]{2,1,0:T(8,128)(2,1)S(1)}) custom-call(s32[3]{0:T(128)S(1)} %bitcast.64, bf16[3,2,256,256]{3,2,1,0:T(8,128)(2,1)S(1)} %bitcast.61, bf16[2,256,256]{2,1,0:T(8,128)(2,1)S(1)} %mask.1.refs_0_), custom_call_target="tpu_custom_call" | custom-call | flops 1 | bytes 1 | tf_op jit(solution)/shard_map/mask_rows/pallas_call | solution.py:536
  7.8 1.6 %collective-permute-start.6 = (bf16[3,256,256]{2,1,0:T(8,128)(2,1)S(1)}, bf16[3,256,256]{2,1,0:T(8,128)(2,1)S(1)}, u32[]{:S(2)}, u32[]{:S(2)}) collective-permute-start(bf16[3,256,256]{2,1,0:T(8,128)(2,1)S(1)} %get-tuple-element.39.refs_0_), channel_id=1, source_target_pairs={{0,4},{4,0},{8,12},{12,8},{1,5},{5,1},{9,13},{13,9},{2,6},{6,2},{1... | collective-permute-start | bytes 1179656 | tf_op jit(solution)/shard_map/ppermute | solution.py:44
  9.4 1.5 %collective-permute-start.7 = (bf16[3,256,256]{2,1,0:T(8,128)(2,1)S(1)}, bf16[3,256,256]{2,1,0:T(8,128)(2,1)S(1)}, u32[]{:S(2)}, u32[]{:S(2)}) collective-permute-start(bf16[3,256,256]{2,1,0:T(8,128)(2,1)S(1)} %get-tuple-element.40.refs_0_.refs_3_), channel_id=1, source_target_pairs={{0,8},{4,12},{8,0},{12,4},{1,9},{5,13},{9,1},{13,5},{2,10},{6,14},... | collective-permute-start | bytes 1179656 | tf_op jit(solution)/shard_map/ppermute | solution.py:44
  11.3 1.6 %collective-permute-done.refs_1_ = bf16[2,256,256]{2,1,0:T(8,128)(2,1)S(1)} collective-permute-done((bf16[2,256,256]{2,1,0:T(8,128)(2,1)S(1)}, bf16[2,256,256]{2,1,0:T(8,128)(2,1)S(1)}, u32[]{:S(2)}, u32[]{:S(2)}) %collective-permute-start) | collective-permute-done | bytes 262176 | tf_op jit(solution)/shard_map/ppermute | solution.py:461
  13.0 0.8 join.5.refs_2_
  13.8 0.7 copy-done.14
  14.5 1.5 %collective-permute-start.1 = (bf16[2,2,256,256]{3,2,1,0:T(8,128)(2,1)}, bf16[2,2,256,256]{3,2,1,0:T(8,128)(2,1)}, u32[]{:S(2)}, u32[]{:S(2)}) collective-permute-start(bf16[2,2,256,256]{3,2,1,0:T(8,128)(2,1)} %join.5.refs_2_), channel_id=1, source_target_pairs={{1,2},{2,1},{5,6},{6,5},{9,10},{10,9},{13,14},{14,13},{17,18},{18,... | collective-permute-start | bytes 1572872 | tf_op jit(solution)/shard_map/ppermute | solution.py:463
  16.0 2.2 %collective-permute-done.4.refs_1_.refs_3_ = bf16[2,256,256]{2,1,0:T(8,128)(2,1)S(1)} collective-permute-done((bf16[2,256,256]{2,1,0:T(8,128)(2,1)S(1)}, bf16[2,256,256]{2,1,0:T(8,128)(2,1)S(1)}, u32[]{:S(2)}, u32[]{:S(2)}) %collective-permute-start.4) | collective-permute-done | bytes 262176 | tf_op jit(solution)/shard_map/ppermute | solution.py:461
  18.5 1.2 collective-permute-done.7.refs_4_.refs_1_.refs_5_
  19.7 0.9 join.6.refs_2_
  20.6 1.5 %collective-permute-start.8 = (bf16[2,2,256,256]{3,2,1,0:T(8,128)(2,1)}, bf16[2,2,256,256]{3,2,1,0:T(8,128)(2,1)}, u32[]{:S(2)}, u32[]{:S(2)}) collective-permute-start(bf16[2,2,256,256]{3,2,1,0:T(8,128)(2,1)} %join.6.refs_2_), channel_id=1, source_target_pairs={{1,2},{2,1},{5,6},{6,5},{9,10},{10,9},{13,14},{14,13},{17,18},{18,... | collective-permute-start | bytes 1572872 | tf_op jit(solution)/shard_map/ppermute | solution.py:463
  22.0 3.6 %collective-permute-start.5 = (bf16[2,256,256]{2,1,0:T(8,128)(2,1)}, bf16[2,256,256]{2,1,0:T(8,128)(2,1)}, u32[]{:S(2)}, u32[]{:S(2)}) collective-permute-start(bf16[2,256,256]{2,1,0:T(8,128)(2,1)} %get-tuple-element.38.refs_4_.refs_0_), channel_id=1, source_target_pairs={{0,1},{1,0},{2,3},{3,2},{4,5},{5,4},{6,7},{7,6},{8,9},{9,8},{10,11... | collective-permute-start | bytes 786440 | tf_op jit(solution)/shard_map/ppermute | solution.py:461
  26.2 1.6 %slice_bitcast_fusion = (f32[2,256,256]{2,1,0:T(8,128)S(1)}, f32[2,256,256]{2,1,0:T(8,128)S(1)}, f32[2,256,256]{2,1,0:T(8,128)S(1)}) fusion(f32[1,3,2,256,256]{4,3,2,1,0:T(8,128)} %param.10), kind=kLoop, calls=%fused_computation.5 | loop fusion | bytes 3145728 | tf_op jit(solution)/shard_map/squeeze | solution.py:639
  27.9 1.6 %collective-permute-start.9 = (bf16[2,3,256,256]{3,2,1,0:T(8,128)(2,1)S(1)}, bf16[2,3,256,256]{3,2,1,0:T(8,128)(2,1)S(1)}, u32[]{:S(2)}, u32[]{:S(2)}) collective-permute-start(bf16[2,3,256,256]{3,2,1,0:T(8,128)(2,1)S(1)} %join.7.refs_3_), channel_id=1, source_target_pairs={{0,8},{4,12},{8,0},{12,4},{1,9},{5,13},{9,1},{13,5},{2,10},{6,14},... | collective-permute-start | bytes 2359304 | tf_op jit(solution)/shard_map/ppermute | solution.py:44
  29.6 0.6 collective-permute-start.10
  30.5 2.3 %join.9 = bf16[2,2,256,256]{3,2,1,0:T(8,128)(2,1)} custom-call(bf16[2,256,256]{2,1,0:T(8,128)(2,1)} %get-tuple-element.38.refs_4_.refs_0_, bf16[2,256,256]{2,1,0:T(8,128)(2,1)} %collective-permute-done.5.refs_5_.refs_1_, bf16[2,2,256,256]{3,2,1,0:T(8,128)(2,1)} %join.6.refs_2_, bf16[2,3,256,256]{3,2,1,0:T(8,128)(2,1)S(1)} %join.7.refs_3_, ...), custom_call_target="tpu_custom_call" | custom-call | flops 1 | bytes 1 | tf_op jit(solution)/shard_map/join/pallas_call | solution.py:382
  32.8 1.5 %collective-permute-start.22 = (bf16[2,2,256,256]{3,2,1,0:T(8,128)(2,1)}, bf16[2,2,256,256]{3,2,1,0:T(8,128)(2,1)}, u32[]{:S(2)}, u32[]{:S(2)}) collective-permute-start(bf16[2,2,256,256]{3,2,1,0:T(8,128)(2,1)} %join.9), channel_id=1, source_target_pairs={{1,2},{2,1},{5,6},{6,5},{9,10},{10,9},{13,14},{14,13},{17,18},{18,... | collective-permute-start | bytes 1572872 | tf_op jit(solution)/shard_map/ppermute | solution.py:463
  34.3 1.9 %slice_bitcast_fusion.3 = (bf16[2,256,256]{2,1,0:T(8,128)(2,1)}, bf16[2,256,256]{2,1,0:T(8,128)(2,1)}) fusion(bf16[2,2,256,256]{3,2,1,0:T(8,128)(2,1)} %collective-permute-done.1.refs_6_.refs_2_), kind=kLoop, calls=%fused_computation.10 | loop fusion | bytes 1048576 | tf_op jit(solution)/shard_map/squeeze | solution.py:465
  36.1 1.3 %collective-permute-start.2 = (bf16[2,256,256]{2,1,0:T(8,128)(2,1)}, bf16[2,256,256]{2,1,0:T(8,128)(2,1)}, u32[]{:S(2)}, u32[]{:S(2)}) collective-permute-start(bf16[2,256,256]{2,1,0:T(8,128)(2,1)} %get-tuple-element.81), channel_id=1, source_target_pairs={{1,0},{2,3},{5,4},{6,7},{9,8},{10,11},{13,12},{14,15},{17,16},{18,... | collective-permute-start | bytes 786440 | tf_op jit(solution)/shard_map/ppermute | solution.py:465
  37.4 1.3 %collective-permute-start.3 = (bf16[2,256,256]{2,1,0:T(8,128)(2,1)}, bf16[2,256,256]{2,1,0:T(8,128)(2,1)}, u32[]{:S(2)}, u32[]{:S(2)}) collective-permute-start(bf16[2,256,256]{2,1,0:T(8,128)(2,1)} %get-tuple-element.80), channel_id=1, source_target_pairs={{1,0},{2,3},{5,4},{6,7},{9,8},{10,11},{13,12},{14,15},{17,16},{18,... | collective-permute-start | bytes 786440 | tf_op jit(solution)/shard_map/ppermute | solution.py:465
  38.8 5.3 %early.1 = (f32[512,1024]{1,0:T(8,128)S(1)}, f32[512,1024]{1,0:T(8,128)S(1)}, f32[512,1024]{1,0:T(8,128)S(1)}, bf16[2,2,256,1024]{3,2,1,0:T(8,128)(2,1)S(1)}) custom-call(s32[8]{0:T(128)S(1)} %stack.79.place_ref.refs_0_, bf16[2,4,256,1024]{3,2,1,0:T(8,128)(2,1)S(1)} %bitcast.65, bf16[2,256,256]{2,1,0:T(8,128)(2,1)S(1)} %mask.1.refs_0_, ...), custom_call_target="tpu_custom_call" | custom-call | flops 99999997952 | bytes 1 | tf_op jit(solution)/shard_map/early/pallas_call | solution.py:188
  44.1 1.1 collective-permute-done.9.refs_2_
  45.2 1.3 %collective-permute-start.16 = (bf16[2,2,256,256]{3,2,1,0:T(8,128)(2,1)}, bf16[2,2,256,256]{3,2,1,0:T(8,128)(2,1)}, u32[]{:S(2)}, u32[]{:S(2)}) collective-permute-start(bf16[2,2,256,256]{3,2,1,0:T(8,128)(2,1)} %collective-permute-done.8.refs_7_.refs_12_.refs_2_), channel_id=1, source_target_pairs={{1,0},{2,3},{5,4},{6,7},{9,8},{10,11},{13,12},{14,15},{17,16},{18,... | collective-permute-start | bytes 1572872 | tf_op jit(solution)/shard_map/ppermute | solution.py:467
  47.0 6.7 %collective-permute-done.3.refs_4_ = bf16[2,256,256]{2,1,0:T(8,128)(2,1)} collective-permute-done((bf16[2,256,256]{2,1,0:T(8,128)(2,1)}, bf16[2,256,256]{2,1,0:T(8,128)(2,1)}, u32[]{:S(2)}, u32[]{:S(2)}) %collective-permute-start.3) | collective-permute-done | bytes 262176 | tf_op jit(solution)/shard_map/ppermute | solution.py:465
  53.8 8.4 %level_0.1 = (f32[512,1024]{1,0:T(8,128)S(1)}, f32[2,256,256]{2,1,0:T(8,128)S(1)}, f32[4,160,256]{2,1,0:T(8,128)S(1)}, f32[2,160,256]{2,1,0:T(8,128)S(1)}, f32[2,160,256]{2,1,0:T(8,128)S(1)}) custom-call(s32[8]{0:T(128)S(1)} %stack.79.place_ref.refs_0_, f32[2]{0:T(128)S(1)} %bitcast.66, ...), custom_call_target="tpu_custom_call", output_to_operand_aliasing={{0}: (9, {})} | custom-call | flops 99999997952 | bytes 1 | tf_op jit(solution)/shard_map/level_0/pallas_call | solution.py:359
  62.2 0.5 collective-permute-start.12
  62.7 1.5 %collective-permute-start.23 = (bf16[2,2,256,256]{3,2,1,0:T(8,128)(2,1)}, bf16[2,2,256,256]{3,2,1,0:T(8,128)(2,1)S(1)}, u32[]{:S(2)}, u32[]{:S(2)}) collective-permute-start(bf16[2,2,256,256]{3,2,1,0:T(8,128)(2,1)} %collective-permute-done.22.refs_2_), channel_id=1, source_target_pairs={{1,0},{2,3},{5,4},{6,7},{9,8},{10,11},{13,12},{14,15},{17,16},{18,... | collective-permute-start | bytes 1572872 | tf_op jit(solution)/shard_map/ppermute | solution.py:467
  64.4 1.6 %collective-permute-start.14 = (f32[1,160,256]{2,1,0:T(8,128)S(1)}, f32[1,160,256]{2,1,0:T(8,128)S(1)}, u32[]{:S(2)}, u32[]{:S(2)}) collective-permute-start(f32[1,160,256]{2,1,0:T(8,128)S(1)} %get-tuple-element.49), channel_id=1, source_target_pairs={{0,8},{4,12},{8,0},{12,4},{1,9},{5,13},{9,1},{13,5},{2,10},{6,14},... | collective-permute-start | bytes 491528 | tf_op jit(solution)/shard_map/ppermute | solution.py:44
  66.0 1.4 %collective-permute-start.15 = (f32[1,160,256]{2,1,0:T(8,128)S(1)}, f32[1,160,256]{2,1,0:T(8,128)S(1)}, u32[]{:S(2)}, u32[]{:S(2)}) collective-permute-start(f32[1,160,256]{2,1,0:T(8,128)S(1)} %get-tuple-element.50), channel_id=1, source_target_pairs={{0,12},{4,8},{8,4},{12,0},{1,13},{5,9},{9,5},{13,1},{2,14},{6,10},... | collective-permute-start | bytes 491528 | tf_op jit(solution)/shard_map/ppermute | solution.py:44
  67.4 0.5 collective-permute-start.13
  67.9 8.3 %level_1.1 = (f32[512,1024]{1,0:T(8,128)S(1)}, f32[2,256,256]{2,1,0:T(8,128)S(1)}, f32[4,160,256]{2,1,0:T(8,128)S(1)}, f32[2,160,256]{2,1,0:T(8,128)S(1)}, f32[2,160,256]{2,1,0:T(8,128)S(1)}) custom-call(s32[8]{0:T(128)S(1)} %stack.79.place_ref.refs_0_, f32[2]{0:T(128)S(1)} %bitcast.67, ...), custom_call_target="tpu_custom_call", output_to_operand_aliasing={{0}: (8, {})} | custom-call | flops 99999997952 | bytes 1 | tf_op jit(solution)/shard_map/level_1/pallas_call | solution.py:359
  76.3 0.5 collective-permute-start.18
  76.9 1.1 collective-permute-done.17.refs_1_
  77.9 0.5 collective-permute-done.18.refs_2_
  78.5 1.6 %collective-permute-start.20 = (f32[1,160,256]{2,1,0:T(8,128)S(1)}, f32[1,160,256]{2,1,0:T(8,128)S(1)}, u32[]{:S(2)}, u32[]{:S(2)}) collective-permute-start(f32[1,160,256]{2,1,0:T(8,128)S(1)} %get-tuple-element.59), channel_id=1, source_target_pairs={{0,8},{4,12},{8,0},{12,4},{1,9},{5,13},{9,1},{13,5},{2,10},{6,14},... | collective-permute-start | bytes 491528 | tf_op jit(solution)/shard_map/ppermute | solution.py:44
  80.1 1.4 %collective-permute-start.21 = (f32[1,160,256]{2,1,0:T(8,128)S(1)}, f32[1,160,256]{2,1,0:T(8,128)S(1)}, u32[]{:S(2)}, u32[]{:S(2)}) collective-permute-start(f32[1,160,256]{2,1,0:T(8,128)S(1)} %get-tuple-element.60), channel_id=1, source_target_pairs={{0,12},{4,8},{8,4},{12,0},{1,13},{5,9},{9,5},{13,1},{2,14},{6,10},... | collective-permute-start | bytes 491528 | tf_op jit(solution)/shard_map/ppermute | solution.py:44
  81.5 0.5 collective-permute-start.19
  82.0 3.6 %level_2.1 = (f32[4,160,256]{2,1,0:T(8,128)S(1)}, f32[2,160,256]{2,1,0:T(8,128)S(1)}, f32[2,160,256]{2,1,0:T(8,128)S(1)}) custom-call(s32[8]{0:T(128)S(1)} %stack.79.place_ref.refs_0_, f32[2]{0:T(128)S(1)} %bitcast.68, bf16[2,2,256,256]{3,2,1,0:T(8,128)(2,1)} %collective-permute-done.22.refs_2_, ...), custom_call_target="tpu_custom_call" | custom-call | flops 99999997952 | bytes 1 | tf_op jit(solution)/shard_map/level_2/pallas_call | solution.py:359
  85.7 2.6 %collective-permute-done.20 = f32[1,160,256]{2,1,0:T(8,128)S(1)} collective-permute-done((f32[1,160,256]{2,1,0:T(8,128)S(1)}, f32[1,160,256]{2,1,0:T(8,128)S(1)}, u32[]{:S(2)}, u32[]{:S(2)}) %collective-permute-start.20) | collective-permute-done | bytes 163872 | tf_op jit(solution)/shard_map/ppermute | solution.py:44
  88.3 1.2 collective-permute-done.19
  89.7 0.5 collective-permute-start.25
  90.2 1.1 collective-permute-done.24.refs_1_
  91.9 1.6 %collective-permute-start.27 = (f32[1,160,256]{2,1,0:T(8,128)S(1)}, f32[1,160,256]{2,1,0:T(8,128)S(1)}, u32[]{:S(2)}, u32[]{:S(2)}) collective-permute-start(f32[1,160,256]{2,1,0:T(8,128)S(1)} %get-tuple-element.70), channel_id=1, source_target_pairs={{0,8},{4,12},{8,0},{12,4},{1,9},{5,13},{9,1},{13,5},{2,10},{6,14},... | collective-permute-start | bytes 491528 | tf_op jit(solution)/shard_map/ppermute | solution.py:44
  93.5 1.4 %collective-permute-start.28 = (f32[1,160,256]{2,1,0:T(8,128)S(1)}, f32[1,160,256]{2,1,0:T(8,128)S(1)}, u32[]{:S(2)}, u32[]{:S(2)}) collective-permute-start(f32[1,160,256]{2,1,0:T(8,128)S(1)} %get-tuple-element.71), channel_id=1, source_target_pairs={{0,12},{4,8},{8,4},{12,0},{1,13},{5,9},{9,5},{13,1},{2,14},{6,10},... | collective-permute-start | bytes 491528 | tf_op jit(solution)/shard_map/ppermute | solution.py:44
  94.9 0.5 collective-permute-start.26
  95.4 6.3 %collective-permute-done.27 = f32[1,160,256]{2,1,0:T(8,128)S(1)} collective-permute-done((f32[1,160,256]{2,1,0:T(8,128)S(1)}, f32[1,160,256]{2,1,0:T(8,128)S(1)}, u32[]{:S(2)}, u32[]{:S(2)}) %collective-permute-start.27) | collective-permute-done | bytes 163872 | tf_op jit(solution)/shard_map/ppermute | solution.py:44
  101.7 1.2 collective-permute-done.26
  103.0 3.5 %collective-permute-start.30 = (f32[3,32,256]{2,1,0:T(8,128)S(1)}, f32[3,32,256]{2,1,0:T(8,128)S(1)}, u32[]{:S(2)}, u32[]{:S(2)}) collective-permute-start(f32[3,32,256]{2,1,0:T(8,128)S(1)} %cut.1), channel_id=1, source_target_pairs={{0,2},{1,3},{2,0},{3,1},{4,6},{5,7},{6,4},{7,5},{8,10},{9,11},{10,... | collective-permute-start | bytes 294920 | tf_op jit(solution)/shard_map/ppermute | solution.py:44
  106.5 1.5 %collective-permute-start.31 = (f32[3,32,256]{2,1,0:T(8,128)S(1)}, f32[3,32,256]{2,1,0:T(8,128)S(1)}, u32[]{:S(2)}, u32[]{:S(2)}) collective-permute-start(f32[3,32,256]{2,1,0:T(8,128)S(1)} %cut.1), channel_id=1, source_target_pairs={{0,3},{1,2},{2,1},{3,0},{4,7},{5,6},{6,5},{7,4},{8,11},{9,10},{10,... | collective-permute-start | bytes 294920 | tf_op jit(solution)/shard_map/ppermute | solution.py:44
  108.0 5.6 %collective-permute-done.30 = f32[3,32,256]{2,1,0:T(8,128)S(1)} collective-permute-done((f32[3,32,256]{2,1,0:T(8,128)S(1)}, f32[3,32,256]{2,1,0:T(8,128)S(1)}, u32[]{:S(2)}, u32[]{:S(2)}) %collective-permute-start.30) | collective-permute-done | bytes 98336 | tf_op jit(solution)/shard_map/ppermute | solution.py:44
  113.9 0.6 collective-permute-done.29
  114.5 2.5 %collective-permute-start.34 = (f32[3,32,256]{2,1,0:T(8,128)S(1)}, f32[3,32,256]{2,1,0:T(8,128)S(1)}, u32[]{:S(2)}, u32[]{:S(2)}) collective-permute-start(f32[3,32,256]{2,1,0:T(8,128)S(1)} %add_add_fusion.3), channel_id=1, source_target_pairs={{0,12},{4,8},{8,4},{12,0},{1,13},{5,9},{9,5},{13,1},{2,14},{6,10},... | collective-permute-start | bytes 294920 | tf_op jit(solution)/shard_map/ppermute | solution.py:44
  117.0 0.5 collective-permute-start.33
  117.5 0.5 collective-permute-start.32
  118.0 2.0 %collective-permute-done.34 = f32[3,32,256]{2,1,0:T(8,128)S(1)} collective-permute-done((f32[3,32,256]{2,1,0:T(8,128)S(1)}, f32[3,32,256]{2,1,0:T(8,128)S(1)}, u32[]{:S(2)}, u32[]{:S(2)}) %collective-permute-start.34) | collective-permute-done | bytes 98336 | tf_op jit(solution)/shard_map/ppermute | solution.py:44
  120.1 1.6 %collective-permute-done.33 = f32[3,32,256]{2,1,0:T(8,128)S(1)} collective-permute-done((f32[3,32,256]{2,1,0:T(8,128)S(1)}, f32[3,32,256]{2,1,0:T(8,128)S(1)}, u32[]{:S(2)}, u32[]{:S(2)}) %collective-permute-start.33) | collective-permute-done | bytes 98336 | tf_op jit(solution)/shard_map/ppermute | solution.py:44
  121.6 0.5 collective-permute-done.32
  122.5 0.9 copy.12
  123.4 0.7 collective-permute-done.35
  124.3 0.9 pad_maximum_fusion.1
  (84 shorter events, 4.2 us)
Async XLA Ops:
  0.6 1.1 copy-start
  1.8 0.7 copy-start.16
  3.1 22.6 %copy-start.5 = (f32[1,2,2,256,256]{4,3,2,1,0:T(8,128)S(1)}, f32[1,2,2,256,256]{4,3,2,1,0:T(8,128)}, u32[]{:S(2)}) copy-start(f32[1,2,2,256,256]{4,3,2,1,0:T(8,128)} %param.9) | copy-start | bytes 3145732
  3.2 9.8 %collective-permute-start = (bf16[2,256,256]{2,1,0:T(8,128)(2,1)S(1)}, bf16[2,256,256]{2,1,0:T(8,128)(2,1)S(1)}, u32[]{:S(2)}, u32[]{:S(2)}) collective-permute-start(bf16[2,256,256]{2,1,0:T(8,128)(2,1)S(1)} %mask.1.refs_0_), channel_id=1, source_target_pairs={{0,1},{1,0},{2,3},{3,2},{4,5},{5,4},{6,7},{7,6},{8,9},{9,8},{10,11... | collective-permute-start | bytes 786440 | tf_op jit(solution)/shard_map/ppermute | solution.py:461
  7.8 10.7 %copy-start.6 = (bf16[3,256,256]{2,1,0:T(8,128)(2,1)}, bf16[3,256,256]{2,1,0:T(8,128)(2,1)S(1)}, u32[]{:S(2)}) copy-start(bf16[3,256,256]{2,1,0:T(8,128)(2,1)S(1)} %get-tuple-element.39.refs_0_) | copy-start | bytes 1179652
  7.8 17.9 %copy-start.8 = (bf16[3,256,256]{2,1,0:T(8,128)(2,1)}, bf16[3,256,256]{2,1,0:T(8,128)(2,1)S(1)}, u32[]{:S(2)}) copy-start(bf16[3,256,256]{2,1,0:T(8,128)(2,1)S(1)} %get-tuple-element.40.refs_0_.refs_3_) | copy-start | bytes 1179652
  7.8 17.9 %copy-start.10 = (bf16[2,256,256]{2,1,0:T(8,128)(2,1)}, bf16[2,256,256]{2,1,0:T(8,128)(2,1)S(1)}, u32[]{:S(2)}) copy-start(bf16[2,256,256]{2,1,0:T(8,128)(2,1)S(1)} %get-tuple-element.37.refs_0_.refs_2_) | copy-start | bytes 786436
  7.8 10.6 %collective-permute-start.6 = (bf16[3,256,256]{2,1,0:T(8,128)(2,1)S(1)}, bf16[3,256,256]{2,1,0:T(8,128)(2,1)S(1)}, u32[]{:S(2)}, u32[]{:S(2)}) collective-permute-start(bf16[3,256,256]{2,1,0:T(8,128)(2,1)S(1)} %get-tuple-element.39.refs_0_), channel_id=1, source_target_pairs={{0,4},{4,0},{8,12},{12,8},{1,5},{5,1},{9,13},{13,9},{2,6},{6,2},{1... | collective-permute-start | bytes 1179656 | tf_op jit(solution)/shard_map/ppermute | solution.py:44
  9.4 10.3 %collective-permute-start.7 = (bf16[3,256,256]{2,1,0:T(8,128)(2,1)S(1)}, bf16[3,256,256]{2,1,0:T(8,128)(2,1)S(1)}, u32[]{:S(2)}, u32[]{:S(2)}) collective-permute-start(bf16[3,256,256]{2,1,0:T(8,128)(2,1)S(1)} %get-tuple-element.40.refs_0_.refs_3_), channel_id=1, source_target_pairs={{0,8},{4,12},{8,0},{12,4},{1,9},{5,13},{9,1},{13,5},{2,10},{6,14},... | collective-permute-start | bytes 1179656 | tf_op jit(solution)/shard_map/ppermute | solution.py:44
  10.9 7.3 %collective-permute-start.4 = (bf16[2,256,256]{2,1,0:T(8,128)(2,1)S(1)}, bf16[2,256,256]{2,1,0:T(8,128)(2,1)S(1)}, u32[]{:S(2)}, u32[]{:S(2)}) collective-permute-start(bf16[2,256,256]{2,1,0:T(8,128)(2,1)S(1)} %get-tuple-element.37.refs_0_.refs_2_), channel_id=1, source_target_pairs={{0,1},{1,0},{2,3},{3,2},{4,5},{5,4},{6,7},{7,6},{8,9},{9,8},{10,11... | collective-permute-start | bytes 786440 | tf_op jit(solution)/shard_map/ppermute | solution.py:461
  13.8 0.7 copy-start.14
  14.5 19.8 %collective-permute-start.1 = (bf16[2,2,256,256]{3,2,1,0:T(8,128)(2,1)}, bf16[2,2,256,256]{3,2,1,0:T(8,128)(2,1)}, u32[]{:S(2)}, u32[]{:S(2)}) collective-permute-start(bf16[2,2,256,256]{3,2,1,0:T(8,128)(2,1)} %join.5.refs_2_), channel_id=1, source_target_pairs={{1,2},{2,1},{5,6},{6,5},{9,10},{10,9},{13,14},{14,13},{17,18},{18,... | collective-permute-start | bytes 1572872 | tf_op jit(solution)/shard_map/ppermute | solution.py:463
  18.2 7.5 %copy-start.12 = (bf16[2,256,256]{2,1,0:T(8,128)(2,1)}, bf16[2,256,256]{2,1,0:T(8,128)(2,1)S(1)}, u32[]{:S(2)}) copy-start(bf16[2,256,256]{2,1,0:T(8,128)(2,1)S(1)} %collective-permute-done.4.refs_1_.refs_3_) | copy-start | bytes 786436
  18.5 7.2 %copy-start.1 = (bf16[3,256,256]{2,1,0:T(8,128)(2,1)}, bf16[3,256,256]{2,1,0:T(8,128)(2,1)S(1)}, u32[]{:S(2)}) copy-start(bf16[3,256,256]{2,1,0:T(8,128)(2,1)S(1)} %collective-permute-done.6.refs_3_.refs_1_) | copy-start | bytes 1179652
  19.7 6.0 %copy-start.3 = (bf16[3,256,256]{2,1,0:T(8,128)(2,1)}, bf16[3,256,256]{2,1,0:T(8,128)(2,1)S(1)}, u32[]{:S(2)}) copy-start(bf16[3,256,256]{2,1,0:T(8,128)(2,1)S(1)} %collective-permute-done.7.refs_4_.refs_1_.refs_5_) | copy-start | bytes 1179652
  20.6 16.9 %collective-permute-start.8 = (bf16[2,2,256,256]{3,2,1,0:T(8,128)(2,1)}, bf16[2,2,256,256]{3,2,1,0:T(8,128)(2,1)}, u32[]{:S(2)}, u32[]{:S(2)}) collective-permute-start(bf16[2,2,256,256]{3,2,1,0:T(8,128)(2,1)} %join.6.refs_2_), channel_id=1, source_target_pairs={{1,2},{2,1},{5,6},{6,5},{9,10},{10,9},{13,14},{14,13},{17,18},{18,... | collective-permute-start | bytes 1572872 | tf_op jit(solution)/shard_map/ppermute | solution.py:463
  22.0 8.5 %collective-permute-start.5 = (bf16[2,256,256]{2,1,0:T(8,128)(2,1)}, bf16[2,256,256]{2,1,0:T(8,128)(2,1)}, u32[]{:S(2)}, u32[]{:S(2)}) collective-permute-start(bf16[2,256,256]{2,1,0:T(8,128)(2,1)} %get-tuple-element.38.refs_4_.refs_0_), channel_id=1, source_target_pairs={{0,1},{1,0},{2,3},{3,2},{4,5},{5,4},{6,7},{7,6},{8,9},{9,8},{10,11... | collective-permute-start | bytes 786440 | tf_op jit(solution)/shard_map/ppermute | solution.py:461
  26.2 1.6 %copy-start.2 = (bf16[3,256,256]{2,1,0:T(8,128)(2,1)S(1)}, bf16[3,256,256]{2,1,0:T(8,128)(2,1)}, u32[]{:S(2)}) copy-start(bf16[3,256,256]{2,1,0:T(8,128)(2,1)} %copy-done.1) | copy-start | bytes 1179652
  26.2 1.6 %copy-start.7 = (bf16[3,256,256]{2,1,0:T(8,128)(2,1)S(1)}, bf16[3,256,256]{2,1,0:T(8,128)(2,1)}, u32[]{:S(2)}) copy-start(bf16[3,256,256]{2,1,0:T(8,128)(2,1)} %copy-done.6) | copy-start | bytes 1179652
  26.2 3.3 %copy-start.4 = (bf16[3,256,256]{2,1,0:T(8,128)(2,1)S(1)}, bf16[3,256,256]{2,1,0:T(8,128)(2,1)}, u32[]{:S(2)}) copy-start(bf16[3,256,256]{2,1,0:T(8,128)(2,1)} %copy-done.3) | copy-start | bytes 1179652
  26.2 3.3 %copy-start.9 = (bf16[3,256,256]{2,1,0:T(8,128)(2,1)S(1)}, bf16[3,256,256]{2,1,0:T(8,128)(2,1)}, u32[]{:S(2)}) copy-start(bf16[3,256,256]{2,1,0:T(8,128)(2,1)} %copy-done.8) | copy-start | bytes 1179652
  27.9 17.3 %collective-permute-start.9 = (bf16[2,3,256,256]{3,2,1,0:T(8,128)(2,1)S(1)}, bf16[2,3,256,256]{3,2,1,0:T(8,128)(2,1)S(1)}, u32[]{:S(2)}, u32[]{:S(2)}) collective-permute-start(bf16[2,3,256,256]{3,2,1,0:T(8,128)(2,1)S(1)} %join.7.refs_3_), channel_id=1, source_target_pairs={{0,8},{4,12},{8,0},{12,4},{1,9},{5,13},{9,1},{13,5},{2,10},{6,14},... | collective-permute-start | bytes 2359304 | tf_op jit(solution)/shard_map/ppermute | solution.py:44
  29.5 9.3 %copy-start.17 = (bf16[1,2,4,1,256,1024]{5,4,3,2,1,0:T(8,128)(2,1)S(1)}, bf16[1,2,4,1,256,1024]{5,4,3,2,1,0:T(8,128)(2,1)}, u32[]{:S(2)}) copy-start(bf16[1,2,4,1,256,1024]{5,4,3,2,1,0:T(8,128)(2,1)} %param.6) | copy-start | bytes 12582916
  29.5 9.2 %copy-start.11 = (bf16[2,256,256]{2,1,0:T(8,128)(2,1)S(1)}, bf16[2,256,256]{2,1,0:T(8,128)(2,1)}, u32[]{:S(2)}) copy-start(bf16[2,256,256]{2,1,0:T(8,128)(2,1)} %copy-done.10) | copy-start | bytes 786436
  29.6 9.2 %copy-start.13 = (bf16[2,256,256]{2,1,0:T(8,128)(2,1)S(1)}, bf16[2,256,256]{2,1,0:T(8,128)(2,1)}, u32[]{:S(2)}) copy-start(bf16[2,256,256]{2,1,0:T(8,128)(2,1)} %copy-done.12) | copy-start | bytes 786436
  29.6 9.2 %copy-start.15 = (bf16[2,256,256]{2,1,0:T(8,128)(2,1)S(1)}, bf16[2,256,256]{2,1,0:T(8,128)(2,1)}, u32[]{:S(2)}) copy-start(bf16[2,256,256]{2,1,0:T(8,128)(2,1)} %copy-done.14) | copy-start | bytes 786436
  29.6 17.0 %collective-permute-start.10 = (bf16[2,3,256,256]{3,2,1,0:T(8,128)(2,1)S(1)}, bf16[2,3,256,256]{3,2,1,0:T(8,128)(2,1)S(1)}, u32[]{:S(2)}, u32[]{:S(2)}) collective-permute-start(bf16[2,3,256,256]{3,2,1,0:T(8,128)(2,1)S(1)} %join.8.refs_4_), channel_id=1, source_target_pairs={{0,4},{4,0},{8,12},{12,8},{1,5},{5,1},{9,13},{13,9},{2,6},{6,2},{1... | collective-permute-start | bytes 2359304 | tf_op jit(solution)/shard_map/ppermute | solution.py:44
  32.8 29.9 %collective-permute-start.22 = (bf16[2,2,256,256]{3,2,1,0:T(8,128)(2,1)}, bf16[2,2,256,256]{3,2,1,0:T(8,128)(2,1)}, u32[]{:S(2)}, u32[]{:S(2)}) collective-permute-start(bf16[2,2,256,256]{3,2,1,0:T(8,128)(2,1)} %join.9), channel_id=1, source_target_pairs={{1,2},{2,1},{5,6},{6,5},{9,10},{10,9},{13,14},{14,13},{17,18},{18,... | collective-permute-start | bytes 1572872 | tf_op jit(solution)/shard_map/ppermute | solution.py:463
  36.1 10.9 %collective-permute-start.2 = (bf16[2,256,256]{2,1,0:T(8,128)(2,1)}, bf16[2,256,256]{2,1,0:T(8,128)(2,1)}, u32[]{:S(2)}, u32[]{:S(2)}) collective-permute-start(bf16[2,256,256]{2,1,0:T(8,128)(2,1)} %get-tuple-element.81), channel_id=1, source_target_pairs={{1,0},{2,3},{5,4},{6,7},{9,8},{10,11},{13,12},{14,15},{17,16},{18,... | collective-permute-start | bytes 786440 | tf_op jit(solution)/shard_map/ppermute | solution.py:465
  37.4 16.3 %collective-permute-start.3 = (bf16[2,256,256]{2,1,0:T(8,128)(2,1)}, bf16[2,256,256]{2,1,0:T(8,128)(2,1)}, u32[]{:S(2)}, u32[]{:S(2)}) collective-permute-start(bf16[2,256,256]{2,1,0:T(8,128)(2,1)} %get-tuple-element.80), channel_id=1, source_target_pairs={{1,0},{2,3},{5,4},{6,7},{9,8},{10,11},{13,12},{14,15},{17,16},{18,... | collective-permute-start | bytes 786440 | tf_op jit(solution)/shard_map/ppermute | solution.py:465
  44.1 9.6 %copy-start.18 = (f32[1,2]{1,0:T(1,128)S(1)}, f32[1,2]{1,0:T(1,128)}, u32[]{:S(2)}) copy-start(f32[1,2]{1,0:T(1,128)} %param.11) | copy-start | bytes 28
  45.2 22.7 %collective-permute-start.16 = (bf16[2,2,256,256]{3,2,1,0:T(8,128)(2,1)}, bf16[2,2,256,256]{3,2,1,0:T(8,128)(2,1)}, u32[]{:S(2)}, u32[]{:S(2)}) collective-permute-start(bf16[2,2,256,256]{3,2,1,0:T(8,128)(2,1)} %collective-permute-done.8.refs_7_.refs_12_.refs_2_), channel_id=1, source_target_pairs={{1,0},{2,3},{5,4},{6,7},{9,8},{10,11},{13,12},{14,15},{17,16},{18,... | collective-permute-start | bytes 1572872 | tf_op jit(solution)/shard_map/ppermute | solution.py:467
  62.1 2.1 %collective-permute-start.11 = (f32[2,160,256]{2,1,0:T(8,128)S(1)}, f32[2,160,256]{2,1,0:T(8,128)S(1)}, u32[]{:S(2)}, u32[]{:S(2)}) collective-permute-start(f32[2,160,256]{2,1,0:T(8,128)S(1)} %get-tuple-element.45), channel_id=1, source_target_pairs={{0,16},{16,0},{1,17},{17,1},{2,18},{18,2},{3,19},{19,3},{4,20},{20... | collective-permute-start | bytes 983048 | tf_op jit(solution)/shard_map/ppermute | solution.py:44
  62.2 2.1 %collective-permute-start.12 = (f32[2,160,256]{2,1,0:T(8,128)S(1)}, f32[2,160,256]{2,1,0:T(8,128)S(1)}, u32[]{:S(2)}, u32[]{:S(2)}) collective-permute-start(f32[2,160,256]{2,1,0:T(8,128)S(1)} %get-tuple-element.46), channel_id=1, source_target_pairs={{0,16},{16,0},{1,17},{17,1},{2,18},{18,2},{3,19},{19,3},{4,20},{20... | collective-permute-start | bytes 983048 | tf_op jit(solution)/shard_map/ppermute | solution.py:44
  62.7 19.3 %collective-permute-start.23 = (bf16[2,2,256,256]{3,2,1,0:T(8,128)(2,1)}, bf16[2,2,256,256]{3,2,1,0:T(8,128)(2,1)S(1)}, u32[]{:S(2)}, u32[]{:S(2)}) collective-permute-start(bf16[2,2,256,256]{3,2,1,0:T(8,128)(2,1)} %collective-permute-done.22.refs_2_), channel_id=1, source_target_pairs={{1,0},{2,3},{5,4},{6,7},{9,8},{10,11},{13,12},{14,15},{17,16},{18,... | collective-permute-start | bytes 1572872 | tf_op jit(solution)/shard_map/ppermute | solution.py:467
  64.4 12.0 %collective-permute-start.14 = (f32[1,160,256]{2,1,0:T(8,128)S(1)}, f32[1,160,256]{2,1,0:T(8,128)S(1)}, u32[]{:S(2)}, u32[]{:S(2)}) collective-permute-start(f32[1,160,256]{2,1,0:T(8,128)S(1)} %get-tuple-element.49), channel_id=1, source_target_pairs={{0,8},{4,12},{8,0},{12,4},{1,9},{5,13},{9,1},{13,5},{2,10},{6,14},... | collective-permute-start | bytes 491528 | tf_op jit(solution)/shard_map/ppermute | solution.py:44
  66.0 10.9 %collective-permute-start.15 = (f32[1,160,256]{2,1,0:T(8,128)S(1)}, f32[1,160,256]{2,1,0:T(8,128)S(1)}, u32[]{:S(2)}, u32[]{:S(2)}) collective-permute-start(f32[1,160,256]{2,1,0:T(8,128)S(1)} %get-tuple-element.50), channel_id=1, source_target_pairs={{0,12},{4,8},{8,4},{12,0},{1,13},{5,9},{9,5},{13,1},{2,14},{6,10},... | collective-permute-start | bytes 491528 | tf_op jit(solution)/shard_map/ppermute | solution.py:44
  67.4 9.4 %collective-permute-start.13 = (f32[1,160,256]{2,1,0:T(8,128)S(1)}, f32[1,160,256]{2,1,0:T(8,128)S(1)}, u32[]{:S(2)}, u32[]{:S(2)}) collective-permute-start(f32[1,160,256]{2,1,0:T(8,128)S(1)} %get-tuple-element.48), channel_id=1, source_target_pairs={{0,4},{4,0},{8,12},{12,8},{1,5},{5,1},{9,13},{13,9},{2,6},{6,2},{1... | collective-permute-start | bytes 491528 | tf_op jit(solution)/shard_map/ppermute | solution.py:44
  76.2 1.7 %collective-permute-start.17 = (f32[2,160,256]{2,1,0:T(8,128)S(1)}, f32[2,160,256]{2,1,0:T(8,128)S(1)}, u32[]{:S(2)}, u32[]{:S(2)}) collective-permute-start(f32[2,160,256]{2,1,0:T(8,128)S(1)} %get-tuple-element.55), channel_id=1, source_target_pairs={{0,16},{16,0},{1,17},{17,1},{2,18},{18,2},{3,19},{19,3},{4,20},{20... | collective-permute-start | bytes 983048 | tf_op jit(solution)/shard_map/ppermute | solution.py:44
  76.3 2.1 %collective-permute-start.18 = (f32[2,160,256]{2,1,0:T(8,128)S(1)}, f32[2,160,256]{2,1,0:T(8,128)S(1)}, u32[]{:S(2)}, u32[]{:S(2)}) collective-permute-start(f32[2,160,256]{2,1,0:T(8,128)S(1)} %get-tuple-element.56), channel_id=1, source_target_pairs={{0,16},{16,0},{1,17},{17,1},{2,18},{18,2},{3,19},{19,3},{4,20},{20... | collective-permute-start | bytes 983048 | tf_op jit(solution)/shard_map/ppermute | solution.py:44
  78.5 9.8 %collective-permute-start.20 = (f32[1,160,256]{2,1,0:T(8,128)S(1)}, f32[1,160,256]{2,1,0:T(8,128)S(1)}, u32[]{:S(2)}, u32[]{:S(2)}) collective-permute-start(f32[1,160,256]{2,1,0:T(8,128)S(1)} %get-tuple-element.59), channel_id=1, source_target_pairs={{0,8},{4,12},{8,0},{12,4},{1,9},{5,13},{9,1},{13,5},{2,10},{6,14},... | collective-permute-start | bytes 491528 | tf_op jit(solution)/shard_map/ppermute | solution.py:44
  80.1 8.2 %collective-permute-start.21 = (f32[1,160,256]{2,1,0:T(8,128)S(1)}, f32[1,160,256]{2,1,0:T(8,128)S(1)}, u32[]{:S(2)}, u32[]{:S(2)}) collective-permute-start(f32[1,160,256]{2,1,0:T(8,128)S(1)} %get-tuple-element.60), channel_id=1, source_target_pairs={{0,12},{4,8},{8,4},{12,0},{1,13},{5,9},{9,5},{13,1},{2,14},{6,10},... | collective-permute-start | bytes 491528 | tf_op jit(solution)/shard_map/ppermute | solution.py:44
  81.5 8.0 %collective-permute-start.19 = (f32[1,160,256]{2,1,0:T(8,128)S(1)}, f32[1,160,256]{2,1,0:T(8,128)S(1)}, u32[]{:S(2)}, u32[]{:S(2)}) collective-permute-start(f32[1,160,256]{2,1,0:T(8,128)S(1)} %get-tuple-element.58), channel_id=1, source_target_pairs={{0,4},{4,0},{8,12},{12,8},{1,5},{5,1},{9,13},{13,9},{2,6},{6,2},{1... | collective-permute-start | bytes 491528 | tf_op jit(solution)/shard_map/ppermute | solution.py:44
  89.6 1.7 %collective-permute-start.24 = (f32[2,160,256]{2,1,0:T(8,128)S(1)}, f32[2,160,256]{2,1,0:T(8,128)S(1)}, u32[]{:S(2)}, u32[]{:S(2)}) collective-permute-start(f32[2,160,256]{2,1,0:T(8,128)S(1)} %get-tuple-element.66), channel_id=1, source_target_pairs={{0,16},{16,0},{1,17},{17,1},{2,18},{18,2},{3,19},{19,3},{4,20},{20... | collective-permute-start | bytes 983048 | tf_op jit(solution)/shard_map/ppermute | solution.py:44
  89.7 2.1 %collective-permute-start.25 = (f32[2,160,256]{2,1,0:T(8,128)S(1)}, f32[2,160,256]{2,1,0:T(8,128)S(1)}, u32[]{:S(2)}, u32[]{:S(2)}) collective-permute-start(f32[2,160,256]{2,1,0:T(8,128)S(1)} %get-tuple-element.67), channel_id=1, source_target_pairs={{0,16},{16,0},{1,17},{17,1},{2,18},{18,2},{3,19},{19,3},{4,20},{20... | collective-permute-start | bytes 983048 | tf_op jit(solution)/shard_map/ppermute | solution.py:44
  91.9 9.8 %collective-permute-start.27 = (f32[1,160,256]{2,1,0:T(8,128)S(1)}, f32[1,160,256]{2,1,0:T(8,128)S(1)}, u32[]{:S(2)}, u32[]{:S(2)}) collective-permute-start(f32[1,160,256]{2,1,0:T(8,128)S(1)} %get-tuple-element.70), channel_id=1, source_target_pairs={{0,8},{4,12},{8,0},{12,4},{1,9},{5,13},{9,1},{13,5},{2,10},{6,14},... | collective-permute-start | bytes 491528 | tf_op jit(solution)/shard_map/ppermute | solution.py:44
  93.5 8.2 %collective-permute-start.28 = (f32[1,160,256]{2,1,0:T(8,128)S(1)}, f32[1,160,256]{2,1,0:T(8,128)S(1)}, u32[]{:S(2)}, u32[]{:S(2)}) collective-permute-start(f32[1,160,256]{2,1,0:T(8,128)S(1)} %get-tuple-element.71), channel_id=1, source_target_pairs={{0,12},{4,8},{8,4},{12,0},{1,13},{5,9},{9,5},{13,1},{2,14},{6,10},... | collective-permute-start | bytes 491528 | tf_op jit(solution)/shard_map/ppermute | solution.py:44
  94.9 8.0 %collective-permute-start.26 = (f32[1,160,256]{2,1,0:T(8,128)S(1)}, f32[1,160,256]{2,1,0:T(8,128)S(1)}, u32[]{:S(2)}, u32[]{:S(2)}) collective-permute-start(f32[1,160,256]{2,1,0:T(8,128)S(1)} %get-tuple-element.69), channel_id=1, source_target_pairs={{0,4},{4,0},{8,12},{12,8},{1,5},{5,1},{9,13},{13,9},{2,6},{6,2},{1... | collective-permute-start | bytes 491528 | tf_op jit(solution)/shard_map/ppermute | solution.py:44
  103.0 10.6 %collective-permute-start.30 = (f32[3,32,256]{2,1,0:T(8,128)S(1)}, f32[3,32,256]{2,1,0:T(8,128)S(1)}, u32[]{:S(2)}, u32[]{:S(2)}) collective-permute-start(f32[3,32,256]{2,1,0:T(8,128)S(1)} %cut.1), channel_id=1, source_target_pairs={{0,2},{1,3},{2,0},{3,1},{4,6},{5,7},{6,4},{7,5},{8,10},{9,11},{10,... | collective-permute-start | bytes 294920 | tf_op jit(solution)/shard_map/ppermute | solution.py:44
  106.5 7.3 %collective-permute-start.31 = (f32[3,32,256]{2,1,0:T(8,128)S(1)}, f32[3,32,256]{2,1,0:T(8,128)S(1)}, u32[]{:S(2)}, u32[]{:S(2)}) collective-permute-start(f32[3,32,256]{2,1,0:T(8,128)S(1)} %cut.1), channel_id=1, source_target_pairs={{0,3},{1,2},{2,1},{3,0},{4,7},{5,6},{6,5},{7,4},{8,11},{9,10},{10,... | collective-permute-start | bytes 294920 | tf_op jit(solution)/shard_map/ppermute | solution.py:44
  108.0 6.5 %collective-permute-start.29 = (f32[3,32,256]{2,1,0:T(8,128)S(1)}, f32[3,32,256]{2,1,0:T(8,128)S(1)}, u32[]{:S(2)}, u32[]{:S(2)}) collective-permute-start(f32[3,32,256]{2,1,0:T(8,128)S(1)} %cut.1), channel_id=1, source_target_pairs={{0,1},{1,0},{2,3},{3,2},{4,5},{5,4},{6,7},{7,6},{8,9},{9,8},{10,11... | collective-permute-start | bytes 294920 | tf_op jit(solution)/shard_map/ppermute | solution.py:44
  114.5 5.6 %collective-permute-start.34 = (f32[3,32,256]{2,1,0:T(8,128)S(1)}, f32[3,32,256]{2,1,0:T(8,128)S(1)}, u32[]{:S(2)}, u32[]{:S(2)}) collective-permute-start(f32[3,32,256]{2,1,0:T(8,128)S(1)} %add_add_fusion.3), channel_id=1, source_target_pairs={{0,12},{4,8},{8,4},{12,0},{1,13},{5,9},{9,5},{13,1},{2,14},{6,10},... | collective-permute-start | bytes 294920 | tf_op jit(solution)/shard_map/ppermute | solution.py:44
  117.0 4.6 %collective-permute-start.33 = (f32[3,32,256]{2,1,0:T(8,128)S(1)}, f32[3,32,256]{2,1,0:T(8,128)S(1)}, u32[]{:S(2)}, u32[]{:S(2)}) collective-permute-start(f32[3,32,256]{2,1,0:T(8,128)S(1)} %add_add_fusion.3), channel_id=1, source_target_pairs={{0,8},{4,12},{8,0},{12,4},{1,9},{5,13},{9,1},{13,5},{2,10},{6,14},... | collective-permute-start | bytes 294920 | tf_op jit(solution)/shard_map/ppermute | solution.py:44
  117.5 4.6 %collective-permute-start.32 = (f32[3,32,256]{2,1,0:T(8,128)S(1)}, f32[3,32,256]{2,1,0:T(8,128)S(1)}, u32[]{:S(2)}, u32[]{:S(2)}) collective-permute-start(f32[3,32,256]{2,1,0:T(8,128)S(1)} %add_add_fusion.3), channel_id=1, source_target_pairs={{0,4},{4,0},{8,12},{12,8},{1,5},{5,1},{9,13},{13,9},{2,6},{6,2},{1... | collective-permute-start | bytes 294920 | tf_op jit(solution)/shard_map/ppermute | solution.py:44
  122.3 1.8 %collective-permute-start.35 = (f32[4,3,32,256]{3,2,0,1:T(8,128)S(1)}, f32[4,3,32,256]{3,2,0,1:T(8,128)S(1)}, u32[]{:S(2)}, u32[]{:S(2)}) collective-permute-start(f32[4,3,32,256]{3,2,0,1:T(8,128)S(1)} %copy.10), channel_id=1, source_target_pairs={{0,16},{16,0},{1,17},{17,1},{2,18},{18,2},{3,19},{19,3},{4,20},{20... | collective-permute-start | bytes 1179656 | tf_op jit(solution)/shard_map/ppermute | solution.py:44
where the time goes:
time: 126 us; the launch traced here: 125 us
  starting transfers between devices  43.2 us (34%)
  waiting for transfers between devices  39.5 us (31%)
  Pallas kernels  33 us (26%)
  local copies, waits for them, and re-layouts  7.12 us (6%)
  other arithmetic  1.34 us (1%)
    ppermute x26, waiting for transfers between devices, exchange(): return lax.ppermute(value, axes, [(i, i ^ distance) for i in range(count)])  28.5 us
    ppermute x26, starting transfers between devices, exchange(): return lax.ppermute(value, axes, [(i, i ^ distance) for i in range(count)])  26.3 us
    pallas_call x3, Pallas kernels, level_products(): pl.pallas_call(kernel, out_shape=outs, in_specs=specs, out_specs=[WHOLE]...  20.3 us
    ppermute x3, starting transfers between devices, gather_four(): near = lax.ppermute(piece, axis, pairs)  7.19 us
    ppermute x2, waiting for transfers between devices, gather_four(): lax.ppermute(middle[n], axis, outer_pairs)  6.81 us
    pallas_call x1, Pallas kernels, early_products(): pl.pallas_call(kernel, out_shape=outs, in_specs=[SCALARS, FAR] + [WHOLE]...  5.32 us
    ppermute x3, starting transfers between devices, gather_four(): middle = lax.ppermute(joined, axis, middle_pairs)  4.41 us
    ppermute x3, waiting for transfers between devices, gather_four(): near = lax.ppermute(piece, axis, pairs)  4.18 us
  transfers between devices with their start and end apart: 36, of which 25 were waited for; matrix products, arithmetic and copies ran while one was open for 4% of the time, Pallas kernels for 26%

commit v1 on v0

--- a/solution.py
+++ b/solution.py
@@ -660,7 +660,8 @@
         if packed:
             panel_parts = [mine[0, :half].T for mine in sums]
             got = spread(cut(sums, half, []))
-            diag_parts = [got[:, :, n].reshape(width, width) for n in range(levels)]
+            diag = jnp.moveaxis(got, 2, 0).reshape(levels, width, width)
+            return jnp.stack(panel_parts)[:, None, None], diag
         return jnp.stack(panel_parts)[:, None, None], jnp.stack(diag_parts)
 
     return per_device

time: 126 us -> 126 us (level)
  no operation moved by 1% of the time
where the time goes in v1:
time: 126 us; the launch traced here: 125 us
  starting transfers between devices  43.2 us (34%)
  waiting for transfers between devices  39.5 us (31%)
  Pallas kernels  33 us (26%)
  local copies, waits for them, and re-layouts  7.05 us (6%)
  other arithmetic  1.27 us (1%)
    ppermute x26, waiting for transfers between devices, exchange(): return lax.ppermute(value, axes, [(i, i ^ distance) for i in range(count)])  28.5 us
    ppermute x26, starting transfers between devices, exchange(): return lax.ppermute(value, axes, [(i, i ^ distance) for i in range(count)])  26.3 us
    pallas_call x3, Pallas kernels, level_products(): pl.pallas_call(kernel, out_shape=outs, in_specs=specs, out_specs=[WHOLE]...  20.3 us
    ppermute x3, starting transfers between devices, gather_four(): near = lax.ppermute(piece, axis, pairs)  7.18 us
    ppermute x2, waiting for transfers between devices, gather_four(): lax.ppermute(middle[n], axis, outer_pairs)  6.8 us
    pallas_call x1, Pallas kernels, early_products(): pl.pallas_call(kernel, out_shape=outs, in_specs=[SCALARS, FAR] + [WHOLE]...  5.32 us
    ppermute x3, starting transfers between devices, gather_four(): middle = lax.ppermute(joined, axis, middle_pairs)  4.41 us
    ppermute x3, waiting for transfers between devices, gather_four(): near = lax.ppermute(piece, axis, pairs)  4.16 us
  transfers between devices with their start and end apart: 36, of which 25 were waited for; matrix products, arithmetic and copies ran while one was open for 4% of the time, Pallas kernels for 26%

profile of v1, /device:TPU:0, one launch (start us, length us, event | category | flops | bytes accessed | tf_op | source)
XLA Modules:
  0.0 125.1 jit_solution(9836735589372156428)
XLA Ops:
  0.6 1.1 copy-done
  1.8 0.7 copy-done.16
  2.4 0.7 mask.1.refs_0_
  3.2 3.1 %collective-permute-start = (bf16[2,256,256]{2,1,0:T(8,128)(2,1)S(1)}, bf16[2,256,256]{2,1,0:T(8,128)(2,1)S(1)}, u32[]{:S(2)}, u32[]{:S(2)}) collective-permute-start(bf16[2,256,256]{2,1,0:T(8,128)(2,1)S(1)} %mask.1.refs_0_), channel_id=1, source_target_pairs={{0,1},{1,0},{2,3},{3,2},{4,5},{5,4},{6,7},{7,6},{8,9},{9,8},{10,11... | collective-permute-start | bytes 786440 | tf_op jit(solution)/shard_map/ppermute | solution.py:461
  6.2 1.5 %mask_rows.1 = (bf16[2,256,256]{2,1,0:T(8,128)(2,1)S(1)}, bf16[2,256,256]{2,1,0:T(8,128)(2,1)}, bf16[3,256,256]{2,1,0:T(8,128)(2,1)S(1)}, bf16[3,256,256]{2,1,0:T(8,128)(2,1)S(1)}) custom-call(s32[3]{0:T(128)S(1)} %bitcast.64, bf16[3,2,256,256]{3,2,1,0:T(8,128)(2,1)S(1)} %bitcast.61, bf16[2,256,256]{2,1,0:T(8,128)(2,1)S(1)} %mask.1.refs_0_), custom_call_target="tpu_custom_call" | custom-call | flops 1 | bytes 1 | tf_op jit(solution)/shard_map/mask_rows/pallas_call | solution.py:536
  7.8 1.6 %collective-permute-start.6 = (bf16[3,256,256]{2,1,0:T(8,128)(2,1)S(1)}, bf16[3,256,256]{2,1,0:T(8,128)(2,1)S(1)}, u32[]{:S(2)}, u32[]{:S(2)}) collective-permute-start(bf16[3,256,256]{2,1,0:T(8,128)(2,1)S(1)} %get-tuple-element.39.refs_0_), channel_id=1, source_target_pairs={{0,4},{4,0},{8,12},{12,8},{1,5},{5,1},{9,13},{13,9},{2,6},{6,2},{1... | collective-permute-start | bytes 1179656 | tf_op jit(solution)/shard_map/ppermute | solution.py:44
  9.4 1.5 %collective-permute-start.7 = (bf16[3,256,256]{2,1,0:T(8,128)(2,1)S(1)}, bf16[3,256,256]{2,1,0:T(8,128)(2,1)S(1)}, u32[]{:S(2)}, u32[]{:S(2)}) collective-permute-start(bf16[3,256,256]{2,1,0:T(8,128)(2,1)S(1)} %get-tuple-element.40.refs_0_.refs_3_), channel_id=1, source_target_pairs={{0,8},{4,12},{8,0},{12,4},{1,9},{5,13},{9,1},{13,5},{2,10},{6,14},... | collective-permute-start | bytes 1179656 | tf_op jit(solution)/shard_map/ppermute | solution.py:44
  11.4 1.6 %collective-permute-done.refs_1_ = bf16[2,256,256]{2,1,0:T(8,128)(2,1)S(1)} collective-permute-done((bf16[2,256,256]{2,1,0:T(8,128)(2,1)S(1)}, bf16[2,256,256]{2,1,0:T(8,128)(2,1)S(1)}, u32[]{:S(2)}, u32[]{:S(2)}) %collective-permute-start) | collective-permute-done | bytes 262176 | tf_op jit(solution)/shard_map/ppermute | solution.py:461
  13.0 0.8 join.5.refs_2_
  13.8 0.7 copy-done.14
  14.5 1.5 %collective-permute-start.1 = (bf16[2,2,256,256]{3,2,1,0:T(8,128)(2,1)}, bf16[2,2,256,256]{3,2,1,0:T(8,128)(2,1)}, u32[]{:S(2)}, u32[]{:S(2)}) collective-permute-start(bf16[2,2,256,256]{3,2,1,0:T(8,128)(2,1)} %join.5.refs_2_), channel_id=1, source_target_pairs={{1,2},{2,1},{5,6},{6,5},{9,10},{10,9},{13,14},{14,13},{17,18},{18,... | collective-permute-start | bytes 1572872 | tf_op jit(solution)/shard_map/ppermute | solution.py:463
  16.0 2.2 %collective-permute-done.4.refs_1_.refs_3_ = bf16[2,256,256]{2,1,0:T(8,128)(2,1)S(1)} collective-permute-done((bf16[2,256,256]{2,1,0:T(8,128)(2,1)S(1)}, bf16[2,256,256]{2,1,0:T(8,128)(2,1)S(1)}, u32[]{:S(2)}, u32[]{:S(2)}) %collective-permute-start.4) | collective-permute-done | bytes 262176 | tf_op jit(solution)/shard_map/ppermute | solution.py:461
  18.5 1.2 collective-permute-done.7.refs_4_.refs_1_.refs_5_
  19.7 0.9 join.6.refs_2_
  20.6 1.5 %collective-permute-start.8 = (bf16[2,2,256,256]{3,2,1,0:T(8,128)(2,1)}, bf16[2,2,256,256]{3,2,1,0:T(8,128)(2,1)}, u32[]{:S(2)}, u32[]{:S(2)}) collective-permute-start(bf16[2,2,256,256]{3,2,1,0:T(8,128)(2,1)} %join.6.refs_2_), channel_id=1, source_target_pairs={{1,2},{2,1},{5,6},{6,5},{9,10},{10,9},{13,14},{14,13},{17,18},{18,... | collective-permute-start | bytes 1572872 | tf_op jit(solution)/shard_map/ppermute | solution.py:463
  22.0 3.6 %collective-permute-start.5 = (bf16[2,256,256]{2,1,0:T(8,128)(2,1)}, bf16[2,256,256]{2,1,0:T(8,128)(2,1)}, u32[]{:S(2)}, u32[]{:S(2)}) collective-permute-start(bf16[2,256,256]{2,1,0:T(8,128)(2,1)} %get-tuple-element.38.refs_4_.refs_0_), channel_id=1, source_target_pairs={{0,1},{1,0},{2,3},{3,2},{4,5},{5,4},{6,7},{7,6},{8,9},{9,8},{10,11... | collective-permute-start | bytes 786440 | tf_op jit(solution)/shard_map/ppermute | solution.py:461
  26.2 1.6 %slice_bitcast_fusion = (f32[2,256,256]{2,1,0:T(8,128)S(1)}, f32[2,256,256]{2,1,0:T(8,128)S(1)}, f32[2,256,256]{2,1,0:T(8,128)S(1)}) fusion(f32[1,3,2,256,256]{4,3,2,1,0:T(8,128)} %param.10), kind=kLoop, calls=%fused_computation.4 | loop fusion | bytes 3145728 | tf_op jit(solution)/shard_map/squeeze | solution.py:639
  27.9 1.6 %collective-permute-start.9 = (bf16[2,3,256,256]{3,2,1,0:T(8,128)(2,1)S(1)}, bf16[2,3,256,256]{3,2,1,0:T(8,128)(2,1)S(1)}, u32[]{:S(2)}, u32[]{:S(2)}) collective-permute-start(bf16[2,3,256,256]{3,2,1,0:T(8,128)(2,1)S(1)} %join.7.refs_3_), channel_id=1, source_target_pairs={{0,8},{4,12},{8,0},{12,4},{1,9},{5,13},{9,1},{13,5},{2,10},{6,14},... | collective-permute-start | bytes 2359304 | tf_op jit(solution)/shard_map/ppermute | solution.py:44
  29.6 0.6 collective-permute-start.10
  30.5 2.3 %join.9 = bf16[2,2,256,256]{3,2,1,0:T(8,128)(2,1)} custom-call(bf16[2,256,256]{2,1,0:T(8,128)(2,1)} %get-tuple-element.38.refs_4_.refs_0_, bf16[2,256,256]{2,1,0:T(8,128)(2,1)} %collective-permute-done.5.refs_5_.refs_1_, bf16[2,2,256,256]{3,2,1,0:T(8,128)(2,1)} %join.6.refs_2_, bf16[2,3,256,256]{3,2,1,0:T(8,128)(2,1)S(1)} %join.7.refs_3_, ...), custom_call_target="tpu_custom_call" | custom-call | flops 1 | bytes 1 | tf_op jit(solution)/shard_map/join/pallas_call | solution.py:382
  32.9 1.5 %collective-permute-start.22 = (bf16[2,2,256,256]{3,2,1,0:T(8,128)(2,1)}, bf16[2,2,256,256]{3,2,1,0:T(8,128)(2,1)}, u32[]{:S(2)}, u32[]{:S(2)}) collective-permute-start(bf16[2,2,256,256]{3,2,1,0:T(8,128)(2,1)} %join.9), channel_id=1, source_target_pairs={{1,2},{2,1},{5,6},{6,5},{9,10},{10,9},{13,14},{14,13},{17,18},{18,... | collective-permute-start | bytes 1572872 | tf_op jit(solution)/shard_map/ppermute | solution.py:463
  34.3 1.9 %slice_bitcast_fusion.3 = (bf16[2,256,256]{2,1,0:T(8,128)(2,1)}, bf16[2,256,256]{2,1,0:T(8,128)(2,1)}) fusion(bf16[2,2,256,256]{3,2,1,0:T(8,128)(2,1)} %collective-permute-done.1.refs_6_.refs_2_), kind=kLoop, calls=%fused_computation.9 | loop fusion | bytes 1048576 | tf_op jit(solution)/shard_map/squeeze | solution.py:465
  36.2 1.3 %collective-permute-start.2 = (bf16[2,256,256]{2,1,0:T(8,128)(2,1)}, bf16[2,256,256]{2,1,0:T(8,128)(2,1)}, u32[]{:S(2)}, u32[]{:S(2)}) collective-permute-start(bf16[2,256,256]{2,1,0:T(8,128)(2,1)} %get-tuple-element.78), channel_id=1, source_target_pairs={{1,0},{2,3},{5,4},{6,7},{9,8},{10,11},{13,12},{14,15},{17,16},{18,... | collective-permute-start | bytes 786440 | tf_op jit(solution)/shard_map/ppermute | solution.py:465
  37.5 1.3 %collective-permute-start.3 = (bf16[2,256,256]{2,1,0:T(8,128)(2,1)}, bf16[2,256,256]{2,1,0:T(8,128)(2,1)}, u32[]{:S(2)}, u32[]{:S(2)}) collective-permute-start(bf16[2,256,256]{2,1,0:T(8,128)(2,1)} %get-tuple-element.77), channel_id=1, source_target_pairs={{1,0},{2,3},{5,4},{6,7},{9,8},{10,11},{13,12},{14,15},{17,16},{18,... | collective-permute-start | bytes 786440 | tf_op jit(solution)/shard_map/ppermute | solution.py:465
  38.8 5.3 %early.1 = (f32[512,1024]{1,0:T(8,128)S(1)}, f32[512,1024]{1,0:T(8,128)S(1)}, f32[512,1024]{1,0:T(8,128)S(1)}, bf16[2,2,256,1024]{3,2,1,0:T(8,128)(2,1)S(1)}) custom-call(s32[8]{0:T(128)S(1)} %stack.76.place_ref.refs_0_, bf16[2,4,256,1024]{3,2,1,0:T(8,128)(2,1)S(1)} %bitcast.65, bf16[2,256,256]{2,1,0:T(8,128)(2,1)S(1)} %mask.1.refs_0_, ...), custom_call_target="tpu_custom_call" | custom-call | flops 99999997952 | bytes 1 | tf_op jit(solution)/shard_map/early/pallas_call | solution.py:188
  44.1 1.1 collective-permute-done.9.refs_2_
  45.2 1.3 %collective-permute-start.16 = (bf16[2,2,256,256]{3,2,1,0:T(8,128)(2,1)}, bf16[2,2,256,256]{3,2,1,0:T(8,128)(2,1)}, u32[]{:S(2)}, u32[]{:S(2)}) collective-permute-start(bf16[2,2,256,256]{3,2,1,0:T(8,128)(2,1)} %collective-permute-done.8.refs_7_.refs_12_.refs_2_), channel_id=1, source_target_pairs={{1,0},{2,3},{5,4},{6,7},{9,8},{10,11},{13,12},{14,15},{17,16},{18,... | collective-permute-start | bytes 1572872 | tf_op jit(solution)/shard_map/ppermute | solution.py:467
  47.0 6.8 %collective-permute-done.3.refs_4_ = bf16[2,256,256]{2,1,0:T(8,128)(2,1)} collective-permute-done((bf16[2,256,256]{2,1,0:T(8,128)(2,1)}, bf16[2,256,256]{2,1,0:T(8,128)(2,1)}, u32[]{:S(2)}, u32[]{:S(2)}) %collective-permute-start.3) | collective-permute-done | bytes 262176 | tf_op jit(solution)/shard_map/ppermute | solution.py:465
  53.8 8.4 %level_0.1 = (f32[512,1024]{1,0:T(8,128)S(1)}, f32[2,256,256]{2,1,0:T(8,128)S(1)}, f32[4,160,256]{2,1,0:T(8,128)S(1)}, f32[2,160,256]{2,1,0:T(8,128)S(1)}, f32[2,160,256]{2,1,0:T(8,128)S(1)}) custom-call(s32[8]{0:T(128)S(1)} %stack.76.place_ref.refs_0_, f32[2]{0:T(128)S(1)} %bitcast.66, ...), custom_call_target="tpu_custom_call", output_to_operand_aliasing={{0}: (9, {})} | custom-call | flops 99999997952 | bytes 1 | tf_op jit(solution)/shard_map/level_0/pallas_call | solution.py:359
  62.2 0.5 collective-permute-start.12
  62.7 1.5 %collective-permute-start.23 = (bf16[2,2,256,256]{3,2,1,0:T(8,128)(2,1)}, bf16[2,2,256,256]{3,2,1,0:T(8,128)(2,1)S(1)}, u32[]{:S(2)}, u32[]{:S(2)}) collective-permute-start(bf16[2,2,256,256]{3,2,1,0:T(8,128)(2,1)} %collective-permute-done.22.refs_2_), channel_id=1, source_target_pairs={{1,0},{2,3},{5,4},{6,7},{9,8},{10,11},{13,12},{14,15},{17,16},{18,... | collective-permute-start | bytes 1572872 | tf_op jit(solution)/shard_map/ppermute | solution.py:467
  64.4 1.6 %collective-permute-start.14 = (f32[1,160,256]{2,1,0:T(8,128)S(1)}, f32[1,160,256]{2,1,0:T(8,128)S(1)}, u32[]{:S(2)}, u32[]{:S(2)}) collective-permute-start(f32[1,160,256]{2,1,0:T(8,128)S(1)} %get-tuple-element.49), channel_id=1, source_target_pairs={{0,8},{4,12},{8,0},{12,4},{1,9},{5,13},{9,1},{13,5},{2,10},{6,14},... | collective-permute-start | bytes 491528 | tf_op jit(solution)/shard_map/ppermute | solution.py:44
  66.0 1.4 %collective-permute-start.15 = (f32[1,160,256]{2,1,0:T(8,128)S(1)}, f32[1,160,256]{2,1,0:T(8,128)S(1)}, u32[]{:S(2)}, u32[]{:S(2)}) collective-permute-start(f32[1,160,256]{2,1,0:T(8,128)S(1)} %get-tuple-element.50), channel_id=1, source_target_pairs={{0,12},{4,8},{8,4},{12,0},{1,13},{5,9},{9,5},{13,1},{2,14},{6,10},... | collective-permute-start | bytes 491528 | tf_op jit(solution)/shard_map/ppermute | solution.py:44
  67.4 0.5 collective-permute-start.13
  67.9 8.3 %level_1.1 = (f32[512,1024]{1,0:T(8,128)S(1)}, f32[2,256,256]{2,1,0:T(8,128)S(1)}, f32[4,160,256]{2,1,0:T(8,128)S(1)}, f32[2,160,256]{2,1,0:T(8,128)S(1)}, f32[2,160,256]{2,1,0:T(8,128)S(1)}) custom-call(s32[8]{0:T(128)S(1)} %stack.76.place_ref.refs_0_, f32[2]{0:T(128)S(1)} %bitcast.67, ...), custom_call_target="tpu_custom_call", output_to_operand_aliasing={{0}: (8, {})} | custom-call | flops 99999997952 | bytes 1 | tf_op jit(solution)/shard_map/level_1/pallas_call | solution.py:359
  76.4 0.5 collective-permute-start.18
  76.9 1.1 collective-permute-done.17.refs_1_
  78.0 0.5 collective-permute-done.18.refs_2_
  78.5 1.6 %collective-permute-start.20 = (f32[1,160,256]{2,1,0:T(8,128)S(1)}, f32[1,160,256]{2,1,0:T(8,128)S(1)}, u32[]{:S(2)}, u32[]{:S(2)}) collective-permute-start(f32[1,160,256]{2,1,0:T(8,128)S(1)} %get-tuple-element.59), channel_id=1, source_target_pairs={{0,8},{4,12},{8,0},{12,4},{1,9},{5,13},{9,1},{13,5},{2,10},{6,14},... | collective-permute-start | bytes 491528 | tf_op jit(solution)/shard_map/ppermute | solution.py:44
  80.1 1.4 %collective-permute-start.21 = (f32[1,160,256]{2,1,0:T(8,128)S(1)}, f32[1,160,256]{2,1,0:T(8,128)S(1)}, u32[]{:S(2)}, u32[]{:S(2)}) collective-permute-start(f32[1,160,256]{2,1,0:T(8,128)S(1)} %get-tuple-element.60), channel_id=1, source_target_pairs={{0,12},{4,8},{8,4},{12,0},{1,13},{5,9},{9,5},{13,1},{2,14},{6,10},... | collective-permute-start | bytes 491528 | tf_op jit(solution)/shard_map/ppermute | solution.py:44
  81.5 0.5 collective-permute-start.19
  82.1 3.6 %level_2.1 = (f32[4,160,256]{2,1,0:T(8,128)S(1)}, f32[2,160,256]{2,1,0:T(8,128)S(1)}, f32[2,160,256]{2,1,0:T(8,128)S(1)}) custom-call(s32[8]{0:T(128)S(1)} %stack.76.place_ref.refs_0_, f32[2]{0:T(128)S(1)} %bitcast.68, bf16[2,2,256,256]{3,2,1,0:T(8,128)(2,1)} %collective-permute-done.22.refs_2_, ...), custom_call_target="tpu_custom_call" | custom-call | flops 99999997952 | bytes 1 | tf_op jit(solution)/shard_map/level_2/pallas_call | solution.py:359
  85.7 2.6 %collective-permute-done.20 = f32[1,160,256]{2,1,0:T(8,128)S(1)} collective-permute-done((f32[1,160,256]{2,1,0:T(8,128)S(1)}, f32[1,160,256]{2,1,0:T(8,128)S(1)}, u32[]{:S(2)}, u32[]{:S(2)}) %collective-permute-start.20) | collective-permute-done | bytes 163872 | tf_op jit(solution)/shard_map/ppermute | solution.py:44
  88.3 1.2 collective-permute-done.19
  89.7 0.5 collective-permute-start.25
  90.2 1.1 collective-permute-done.24.refs_1_
  91.9 1.6 %collective-permute-start.27 = (f32[1,160,256]{2,1,0:T(8,128)S(1)}, f32[1,160,256]{2,1,0:T(8,128)S(1)}, u32[]{:S(2)}, u32[]{:S(2)}) collective-permute-start(f32[1,160,256]{2,1,0:T(8,128)S(1)} %get-tuple-element.70), channel_id=1, source_target_pairs={{0,8},{4,12},{8,0},{12,4},{1,9},{5,13},{9,1},{13,5},{2,10},{6,14},... | collective-permute-start | bytes 491528 | tf_op jit(solution)/shard_map/ppermute | solution.py:44
  93.5 1.4 %collective-permute-start.28 = (f32[1,160,256]{2,1,0:T(8,128)S(1)}, f32[1,160,256]{2,1,0:T(8,128)S(1)}, u32[]{:S(2)}, u32[]{:S(2)}) collective-permute-start(f32[1,160,256]{2,1,0:T(8,128)S(1)} %get-tuple-element.71), channel_id=1, source_target_pairs={{0,12},{4,8},{8,4},{12,0},{1,13},{5,9},{9,5},{13,1},{2,14},{6,10},... | collective-permute-start | bytes 491528 | tf_op jit(solution)/shard_map/ppermute | solution.py:44
  94.9 0.5 collective-permute-start.26
  95.4 6.3 %collective-permute-done.27 = f32[1,160,256]{2,1,0:T(8,128)S(1)} collective-permute-done((f32[1,160,256]{2,1,0:T(8,128)S(1)}, f32[1,160,256]{2,1,0:T(8,128)S(1)}, u32[]{:S(2)}, u32[]{:S(2)}) %collective-permute-start.27) | collective-permute-done | bytes 163872 | tf_op jit(solution)/shard_map/ppermute | solution.py:44
  101.7 1.2 collective-permute-done.26
  103.0 3.5 %collective-permute-start.30 = (f32[3,32,256]{2,1,0:T(8,128)S(1)}, f32[3,32,256]{2,1,0:T(8,128)S(1)}, u32[]{:S(2)}, u32[]{:S(2)}) collective-permute-start(f32[3,32,256]{2,1,0:T(8,128)S(1)} %cut.1), channel_id=1, source_target_pairs={{0,2},{1,3},{2,0},{3,1},{4,6},{5,7},{6,4},{7,5},{8,10},{9,11},{10,... | collective-permute-start | bytes 294920 | tf_op jit(solution)/shard_map/ppermute | solution.py:44
  106.5 1.5 %collective-permute-start.31 = (f32[3,32,256]{2,1,0:T(8,128)S(1)}, f32[3,32,256]{2,1,0:T(8,128)S(1)}, u32[]{:S(2)}, u32[]{:S(2)}) collective-permute-start(f32[3,32,256]{2,1,0:T(8,128)S(1)} %cut.1), channel_id=1, source_target_pairs={{0,3},{1,2},{2,1},{3,0},{4,7},{5,6},{6,5},{7,4},{8,11},{9,10},{10,... | collective-permute-start | bytes 294920 | tf_op jit(solution)/shard_map/ppermute | solution.py:44
  108.0 5.5 %collective-permute-done.30 = f32[3,32,256]{2,1,0:T(8,128)S(1)} collective-permute-done((f32[3,32,256]{2,1,0:T(8,128)S(1)}, f32[3,32,256]{2,1,0:T(8,128)S(1)}, u32[]{:S(2)}, u32[]{:S(2)}) %collective-permute-start.30) | collective-permute-done | bytes 98336 | tf_op jit(solution)/shard_map/ppermute | solution.py:44
  113.8 0.6 collective-permute-done.29
  114.5 2.5 %collective-permute-start.34 = (f32[3,32,256]{2,1,0:T(8,128)S(1)}, f32[3,32,256]{2,1,0:T(8,128)S(1)}, u32[]{:S(2)}, u32[]{:S(2)}) collective-permute-start(f32[3,32,256]{2,1,0:T(8,128)S(1)} %add_add_fusion.3), channel_id=1, source_target_pairs={{0,12},{4,8},{8,4},{12,0},{1,13},{5,9},{9,5},{13,1},{2,14},{6,10},... | collective-permute-start | bytes 294920 | tf_op jit(solution)/shard_map/ppermute | solution.py:44
  117.0 0.5 collective-permute-start.33
  117.5 0.5 collective-permute-start.32
  118.1 2.0 %collective-permute-done.34 = f32[3,32,256]{2,1,0:T(8,128)S(1)} collective-permute-done((f32[3,32,256]{2,1,0:T(8,128)S(1)}, f32[3,32,256]{2,1,0:T(8,128)S(1)}, u32[]{:S(2)}, u32[]{:S(2)}) %collective-permute-start.34) | collective-permute-done | bytes 98336 | tf_op jit(solution)/shard_map/ppermute | solution.py:44
  120.1 1.6 %collective-permute-done.33 = f32[3,32,256]{2,1,0:T(8,128)S(1)} collective-permute-done((f32[3,32,256]{2,1,0:T(8,128)S(1)}, f32[3,32,256]{2,1,0:T(8,128)S(1)}, u32[]{:S(2)}, u32[]{:S(2)}) %collective-permute-start.33) | collective-permute-done | bytes 98336 | tf_op jit(solution)/shard_map/ppermute | solution.py:44
  121.6 0.5 collective-permute-done.32
  122.4 0.9 copy.12
  123.4 0.7 collective-permute-done.35
  124.1 0.9 reverse_select_fusion
  (82 shorter events, 4.1 us)
Async XLA Ops:
  0.6 1.1 copy-start
  1.8 0.7 copy-start.16
  3.1 22.6 %copy-start.5 = (f32[1,2,2,256,256]{4,3,2,1,0:T(8,128)S(1)}, f32[1,2,2,256,256]{4,3,2,1,0:T(8,128)}, u32[]{:S(2)}) copy-start(f32[1,2,2,256,256]{4,3,2,1,0:T(8,128)} %param.9) | copy-start | bytes 3145732
  3.2 9.8 %collective-permute-start = (bf16[2,256,256]{2,1,0:T(8,128)(2,1)S(1)}, bf16[2,256,256]{2,1,0:T(8,128)(2,1)S(1)}, u32[]{:S(2)}, u32[]{:S(2)}) collective-permute-start(bf16[2,256,256]{2,1,0:T(8,128)(2,1)S(1)} %mask.1.refs_0_), channel_id=1, source_target_pairs={{0,1},{1,0},{2,3},{3,2},{4,5},{5,4},{6,7},{7,6},{8,9},{9,8},{10,11... | collective-permute-start | bytes 786440 | tf_op jit(solution)/shard_map/ppermute | solution.py:461
  7.8 10.7 %copy-start.6 = (bf16[3,256,256]{2,1,0:T(8,128)(2,1)}, bf16[3,256,256]{2,1,0:T(8,128)(2,1)S(1)}, u32[]{:S(2)}) copy-start(bf16[3,256,256]{2,1,0:T(8,128)(2,1)S(1)} %get-tuple-element.39.refs_0_) | copy-start | bytes 1179652
  7.8 17.9 %copy-start.8 = (bf16[3,256,256]{2,1,0:T(8,128)(2,1)}, bf16[3,256,256]{2,1,0:T(8,128)(2,1)S(1)}, u32[]{:S(2)}) copy-start(bf16[3,256,256]{2,1,0:T(8,128)(2,1)S(1)} %get-tuple-element.40.refs_0_.refs_3_) | copy-start | bytes 1179652
  7.8 17.9 %copy-start.10 = (bf16[2,256,256]{2,1,0:T(8,128)(2,1)}, bf16[2,256,256]{2,1,0:T(8,128)(2,1)S(1)}, u32[]{:S(2)}) copy-start(bf16[2,256,256]{2,1,0:T(8,128)(2,1)S(1)} %get-tuple-element.37.refs_0_.refs_2_) | copy-start | bytes 786436
  7.8 10.6 %collective-permute-start.6 = (bf16[3,256,256]{2,1,0:T(8,128)(2,1)S(1)}, bf16[3,256,256]{2,1,0:T(8,128)(2,1)S(1)}, u32[]{:S(2)}, u32[]{:S(2)}) collective-permute-start(bf16[3,256,256]{2,1,0:T(8,128)(2,1)S(1)} %get-tuple-element.39.refs_0_), channel_id=1, source_target_pairs={{0,4},{4,0},{8,12},{12,8},{1,5},{5,1},{9,13},{13,9},{2,6},{6,2},{1... | collective-permute-start | bytes 1179656 | tf_op jit(solution)/shard_map/ppermute | solution.py:44
  9.4 10.3 %collective-permute-start.7 = (bf16[3,256,256]{2,1,0:T(8,128)(2,1)S(1)}, bf16[3,256,256]{2,1,0:T(8,128)(2,1)S(1)}, u32[]{:S(2)}, u32[]{:S(2)}) collective-permute-start(bf16[3,256,256]{2,1,0:T(8,128)(2,1)S(1)} %get-tuple-element.40.refs_0_.refs_3_), channel_id=1, source_target_pairs={{0,8},{4,12},{8,0},{12,4},{1,9},{5,13},{9,1},{13,5},{2,10},{6,14},... | collective-permute-start | bytes 1179656 | tf_op jit(solution)/shard_map/ppermute | solution.py:44
  10.9 7.3 %collective-permute-start.4 = (bf16[2,256,256]{2,1,0:T(8,128)(2,1)S(1)}, bf16[2,256,256]{2,1,0:T(8,128)(2,1)S(1)}, u32[]{:S(2)}, u32[]{:S(2)}) collective-permute-start(bf16[2,256,256]{2,1,0:T(8,128)(2,1)S(1)} %get-tuple-element.37.refs_0_.refs_2_), channel_id=1, source_target_pairs={{0,1},{1,0},{2,3},{3,2},{4,5},{5,4},{6,7},{7,6},{8,9},{9,8},{10,11... | collective-permute-start | bytes 786440 | tf_op jit(solution)/shard_map/ppermute | solution.py:461
  13.8 0.7 copy-start.14
  14.5 19.8 %collective-permute-start.1 = (bf16[2,2,256,256]{3,2,1,0:T(8,128)(2,1)}, bf16[2,2,256,256]{3,2,1,0:T(8,128)(2,1)}, u32[]{:S(2)}, u32[]{:S(2)}) collective-permute-start(bf16[2,2,256,256]{3,2,1,0:T(8,128)(2,1)} %join.5.refs_2_), channel_id=1, source_target_pairs={{1,2},{2,1},{5,6},{6,5},{9,10},{10,9},{13,14},{14,13},{17,18},{18,... | collective-permute-start | bytes 1572872 | tf_op jit(solution)/shard_map/ppermute | solution.py:463
  18.2 7.5 %copy-start.12 = (bf16[2,256,256]{2,1,0:T(8,128)(2,1)}, bf16[2,256,256]{2,1,0:T(8,128)(2,1)S(1)}, u32[]{:S(2)}) copy-start(bf16[2,256,256]{2,1,0:T(8,128)(2,1)S(1)} %collective-permute-done.4.refs_1_.refs_3_) | copy-start | bytes 786436
  18.5 7.2 %copy-start.1 = (bf16[3,256,256]{2,1,0:T(8,128)(2,1)}, bf16[3,256,256]{2,1,0:T(8,128)(2,1)S(1)}, u32[]{:S(2)}) copy-start(bf16[3,256,256]{2,1,0:T(8,128)(2,1)S(1)} %collective-permute-done.6.refs_3_.refs_1_) | copy-start | bytes 1179652
  19.7 6.0 %copy-start.3 = (bf16[3,256,256]{2,1,0:T(8,128)(2,1)}, bf16[3,256,256]{2,1,0:T(8,128)(2,1)S(1)}, u32[]{:S(2)}) copy-start(bf16[3,256,256]{2,1,0:T(8,128)(2,1)S(1)} %collective-permute-done.7.refs_4_.refs_1_.refs_5_) | copy-start | bytes 1179652
  20.6 16.9 %collective-permute-start.8 = (bf16[2,2,256,256]{3,2,1,0:T(8,128)(2,1)}, bf16[2,2,256,256]{3,2,1,0:T(8,128)(2,1)}, u32[]{:S(2)}, u32[]{:S(2)}) collective-permute-start(bf16[2,2,256,256]{3,2,1,0:T(8,128)(2,1)} %join.6.refs_2_), channel_id=1, source_target_pairs={{1,2},{2,1},{5,6},{6,5},{9,10},{10,9},{13,14},{14,13},{17,18},{18,... | collective-permute-start | bytes 1572872 | tf_op jit(solution)/shard_map/ppermute | solution.py:463
  22.0 8.5 %collective-permute-start.5 = (bf16[2,256,256]{2,1,0:T(8,128)(2,1)}, bf16[2,256,256]{2,1,0:T(8,128)(2,1)}, u32[]{:S(2)}, u32[]{:S(2)}) collective-permute-start(bf16[2,256,256]{2,1,0:T(8,128)(2,1)} %get-tuple-element.38.refs_4_.refs_0_), channel_id=1, source_target_pairs={{0,1},{1,0},{2,3},{3,2},{4,5},{5,4},{6,7},{7,6},{8,9},{9,8},{10,11... | collective-permute-start | bytes 786440 | tf_op jit(solution)/shard_map/ppermute | solution.py:461
  26.2 1.6 %copy-start.2 = (bf16[3,256,256]{2,1,0:T(8,128)(2,1)S(1)}, bf16[3,256,256]{2,1,0:T(8,128)(2,1)}, u32[]{:S(2)}) copy-start(bf16[3,256,256]{2,1,0:T(8,128)(2,1)} %copy-done.1) | copy-start | bytes 1179652
  26.2 1.6 %copy-start.7 = (bf16[3,256,256]{2,1,0:T(8,128)(2,1)S(1)}, bf16[3,256,256]{2,1,0:T(8,128)(2,1)}, u32[]{:S(2)}) copy-start(bf16[3,256,256]{2,1,0:T(8,128)(2,1)} %copy-done.6) | copy-start | bytes 1179652
  26.2 3.3 %copy-start.4 = (bf16[3,256,256]{2,1,0:T(8,128)(2,1)S(1)}, bf16[3,256,256]{2,1,0:T(8,128)(2,1)}, u32[]{:S(2)}) copy-start(bf16[3,256,256]{2,1,0:T(8,128)(2,1)} %copy-done.3) | copy-start | bytes 1179652
  26.2 3.3 %copy-start.9 = (bf16[3,256,256]{2,1,0:T(8,128)(2,1)S(1)}, bf16[3,256,256]{2,1,0:T(8,128)(2,1)}, u32[]{:S(2)}) copy-start(bf16[3,256,256]{2,1,0:T(8,128)(2,1)} %copy-done.8) | copy-start | bytes 1179652
  27.9 17.3 %collective-permute-start.9 = (bf16[2,3,256,256]{3,2,1,0:T(8,128)(2,1)S(1)}, bf16[2,3,256,256]{3,2,1,0:T(8,128)(2,1)S(1)}, u32[]{:S(2)}, u32[]{:S(2)}) collective-permute-start(bf16[2,3,256,256]{3,2,1,0:T(8,128)(2,1)S(1)} %join.7.refs_3_), channel_id=1, source_target_pairs={{0,8},{4,12},{8,0},{12,4},{1,9},{5,13},{9,1},{13,5},{2,10},{6,14},... | collective-permute-start | bytes 2359304 | tf_op jit(solution)/shard_map/ppermute | solution.py:44
  29.5 9.3 %copy-start.17 = (bf16[1,2,4,1,256,1024]{5,4,3,2,1,0:T(8,128)(2,1)S(1)}, bf16[1,2,4,1,256,1024]{5,4,3,2,1,0:T(8,128)(2,1)}, u32[]{:S(2)}) copy-start(bf16[1,2,4,1,256,1024]{5,4,3,2,1,0:T(8,128)(2,1)} %param.6) | copy-start | bytes 12582916
  29.6 9.2 %copy-start.11 = (bf16[2,256,256]{2,1,0:T(8,128)(2,1)S(1)}, bf16[2,256,256]{2,1,0:T(8,128)(2,1)}, u32[]{:S(2)}) copy-start(bf16[2,256,256]{2,1,0:T(8,128)(2,1)} %copy-done.10) | copy-start | bytes 786436
  29.6 9.2 %copy-start.13 = (bf16[2,256,256]{2,1,0:T(8,128)(2,1)S(1)}, bf16[2,256,256]{2,1,0:T(8,128)(2,1)}, u32[]{:S(2)}) copy-start(bf16[2,256,256]{2,1,0:T(8,128)(2,1)} %copy-done.12) | copy-start | bytes 786436
  29.6 9.2 %copy-start.15 = (bf16[2,256,256]{2,1,0:T(8,128)(2,1)S(1)}, bf16[2,256,256]{2,1,0:T(8,128)(2,1)}, u32[]{:S(2)}) copy-start(bf16[2,256,256]{2,1,0:T(8,128)(2,1)} %copy-done.14) | copy-start | bytes 786436
  29.6 17.0 %collective-permute-start.10 = (bf16[2,3,256,256]{3,2,1,0:T(8,128)(2,1)S(1)}, bf16[2,3,256,256]{3,2,1,0:T(8,128)(2,1)S(1)}, u32[]{:S(2)}, u32[]{:S(2)}) collective-permute-start(bf16[2,3,256,256]{3,2,1,0:T(8,128)(2,1)S(1)} %join.8.refs_4_), channel_id=1, source_target_pairs={{0,4},{4,0},{8,12},{12,8},{1,5},{5,1},{9,13},{13,9},{2,6},{6,2},{1... | collective-permute-start | bytes 2359304 | tf_op jit(solution)/shard_map/ppermute | solution.py:44
  32.9 29.9 %collective-permute-start.22 = (bf16[2,2,256,256]{3,2,1,0:T(8,128)(2,1)}, bf16[2,2,256,256]{3,2,1,0:T(8,128)(2,1)}, u32[]{:S(2)}, u32[]{:S(2)}) collective-permute-start(bf16[2,2,256,256]{3,2,1,0:T(8,128)(2,1)} %join.9), channel_id=1, source_target_pairs={{1,2},{2,1},{5,6},{6,5},{9,10},{10,9},{13,14},{14,13},{17,18},{18,... | collective-permute-start | bytes 1572872 | tf_op jit(solution)/shard_map/ppermute | solution.py:463
  36.2 10.8 %collective-permute-start.2 = (bf16[2,256,256]{2,1,0:T(8,128)(2,1)}, bf16[2,256,256]{2,1,0:T(8,128)(2,1)}, u32[]{:S(2)}, u32[]{:S(2)}) collective-permute-start(bf16[2,256,256]{2,1,0:T(8,128)(2,1)} %get-tuple-element.78), channel_id=1, source_target_pairs={{1,0},{2,3},{5,4},{6,7},{9,8},{10,11},{13,12},{14,15},{17,16},{18,... | collective-permute-start | bytes 786440 | tf_op jit(solution)/shard_map/ppermute | solution.py:465
  37.5 16.3 %collective-permute-start.3 = (bf16[2,256,256]{2,1,0:T(8,128)(2,1)}, bf16[2,256,256]{2,1,0:T(8,128)(2,1)}, u32[]{:S(2)}, u32[]{:S(2)}) collective-permute-start(bf16[2,256,256]{2,1,0:T(8,128)(2,1)} %get-tuple-element.77), channel_id=1, source_target_pairs={{1,0},{2,3},{5,4},{6,7},{9,8},{10,11},{13,12},{14,15},{17,16},{18,... | collective-permute-start | bytes 786440 | tf_op jit(solution)/shard_map/ppermute | solution.py:465
  44.1 9.6 %copy-start.18 = (f32[1,2]{1,0:T(1,128)S(1)}, f32[1,2]{1,0:T(1,128)}, u32[]{:S(2)}) copy-start(f32[1,2]{1,0:T(1,128)} %param.11) | copy-start | bytes 28
  45.2 22.7 %collective-permute-start.16 = (bf16[2,2,256,256]{3,2,1,0:T(8,128)(2,1)}, bf16[2,2,256,256]{3,2,1,0:T(8,128)(2,1)}, u32[]{:S(2)}, u32[]{:S(2)}) collective-permute-start(bf16[2,2,256,256]{3,2,1,0:T(8,128)(2,1)} %collective-permute-done.8.refs_7_.refs_12_.refs_2_), channel_id=1, source_target_pairs={{1,0},{2,3},{5,4},{6,7},{9,8},{10,11},{13,12},{14,15},{17,16},{18,... | collective-permute-start | bytes 1572872 | tf_op jit(solution)/shard_map/ppermute | solution.py:467
  62.1 2.1 %collective-permute-start.11 = (f32[2,160,256]{2,1,0:T(8,128)S(1)}, f32[2,160,256]{2,1,0:T(8,128)S(1)}, u32[]{:S(2)}, u32[]{:S(2)}) collective-permute-start(f32[2,160,256]{2,1,0:T(8,128)S(1)} %get-tuple-element.45), channel_id=1, source_target_pairs={{0,16},{16,0},{1,17},{17,1},{2,18},{18,2},{3,19},{19,3},{4,20},{20... | collective-permute-start | bytes 983048 | tf_op jit(solution)/shard_map/ppermute | solution.py:44
  62.2 2.1 %collective-permute-start.12 = (f32[2,160,256]{2,1,0:T(8,128)S(1)}, f32[2,160,256]{2,1,0:T(8,128)S(1)}, u32[]{:S(2)}, u32[]{:S(2)}) collective-permute-start(f32[2,160,256]{2,1,0:T(8,128)S(1)} %get-tuple-element.46), channel_id=1, source_target_pairs={{0,16},{16,0},{1,17},{17,1},{2,18},{18,2},{3,19},{19,3},{4,20},{20... | collective-permute-start | bytes 983048 | tf_op jit(solution)/shard_map/ppermute | solution.py:44
  62.7 19.3 %collective-permute-start.23 = (bf16[2,2,256,256]{3,2,1,0:T(8,128)(2,1)}, bf16[2,2,256,256]{3,2,1,0:T(8,128)(2,1)S(1)}, u32[]{:S(2)}, u32[]{:S(2)}) collective-permute-start(bf16[2,2,256,256]{3,2,1,0:T(8,128)(2,1)} %collective-permute-done.22.refs_2_), channel_id=1, source_target_pairs={{1,0},{2,3},{5,4},{6,7},{9,8},{10,11},{13,12},{14,15},{17,16},{18,... | collective-permute-start | bytes 1572872 | tf_op jit(solution)/shard_map/ppermute | solution.py:467
  64.4 12.0 %collective-permute-start.14 = (f32[1,160,256]{2,1,0:T(8,128)S(1)}, f32[1,160,256]{2,1,0:T(8,128)S(1)}, u32[]{:S(2)}, u32[]{:S(2)}) collective-permute-start(f32[1,160,256]{2,1,0:T(8,128)S(1)} %get-tuple-element.49), channel_id=1, source_target_pairs={{0,8},{4,12},{8,0},{12,4},{1,9},{5,13},{9,1},{13,5},{2,10},{6,14},... | collective-permute-start | bytes 491528 | tf_op jit(solution)/shard_map/ppermute | solution.py:44
  66.0 10.9 %collective-permute-start.15 = (f32[1,160,256]{2,1,0:T(8,128)S(1)}, f32[1,160,256]{2,1,0:T(8,128)S(1)}, u32[]{:S(2)}, u32[]{:S(2)}) collective-permute-start(f32[1,160,256]{2,1,0:T(8,128)S(1)} %get-tuple-element.50), channel_id=1, source_target_pairs={{0,12},{4,8},{8,4},{12,0},{1,13},{5,9},{9,5},{13,1},{2,14},{6,10},... | collective-permute-start | bytes 491528 | tf_op jit(solution)/shard_map/ppermute | solution.py:44
  67.4 9.5 %collective-permute-start.13 = (f32[1,160,256]{2,1,0:T(8,128)S(1)}, f32[1,160,256]{2,1,0:T(8,128)S(1)}, u32[]{:S(2)}, u32[]{:S(2)}) collective-permute-start(f32[1,160,256]{2,1,0:T(8,128)S(1)} %get-tuple-element.48), channel_id=1, source_target_pairs={{0,4},{4,0},{8,12},{12,8},{1,5},{5,1},{9,13},{13,9},{2,6},{6,2},{1... | collective-permute-start | bytes 491528 | tf_op jit(solution)/shard_map/ppermute | solution.py:44
  76.3 1.7 %collective-permute-start.17 = (f32[2,160,256]{2,1,0:T(8,128)S(1)}, f32[2,160,256]{2,1,0:T(8,128)S(1)}, u32[]{:S(2)}, u32[]{:S(2)}) collective-permute-start(f32[2,160,256]{2,1,0:T(8,128)S(1)} %get-tuple-element.55), channel_id=1, source_target_pairs={{0,16},{16,0},{1,17},{17,1},{2,18},{18,2},{3,19},{19,3},{4,20},{20... | collective-permute-start | bytes 983048 | tf_op jit(solution)/shard_map/ppermute | solution.py:44
  76.4 2.1 %collective-permute-start.18 = (f32[2,160,256]{2,1,0:T(8,128)S(1)}, f32[2,160,256]{2,1,0:T(8,128)S(1)}, u32[]{:S(2)}, u32[]{:S(2)}) collective-permute-start(f32[2,160,256]{2,1,0:T(8,128)S(1)} %get-tuple-element.56), channel_id=1, source_target_pairs={{0,16},{16,0},{1,17},{17,1},{2,18},{18,2},{3,19},{19,3},{4,20},{20... | collective-permute-start | bytes 983048 | tf_op jit(solution)/shard_map/ppermute | solution.py:44
  78.5 9.8 %collective-permute-start.20 = (f32[1,160,256]{2,1,0:T(8,128)S(1)}, f32[1,160,256]{2,1,0:T(8,128)S(1)}, u32[]{:S(2)}, u32[]{:S(2)}) collective-permute-start(f32[1,160,256]{2,1,0:T(8,128)S(1)} %get-tuple-element.59), channel_id=1, source_target_pairs={{0,8},{4,12},{8,0},{12,4},{1,9},{5,13},{9,1},{13,5},{2,10},{6,14},... | collective-permute-start | bytes 491528 | tf_op jit(solution)/shard_map/ppermute | solution.py:44
  80.1 8.2 %collective-permute-start.21 = (f32[1,160,256]{2,1,0:T(8,128)S(1)}, f32[1,160,256]{2,1,0:T(8,128)S(1)}, u32[]{:S(2)}, u32[]{:S(2)}) collective-permute-start(f32[1,160,256]{2,1,0:T(8,128)S(1)} %get-tuple-element.60), channel_id=1, source_target_pairs={{0,12},{4,8},{8,4},{12,0},{1,13},{5,9},{9,5},{13,1},{2,14},{6,10},... | collective-permute-start | bytes 491528 | tf_op jit(solution)/shard_map/ppermute | solution.py:44
  81.5 8.0 %collective-permute-start.19 = (f32[1,160,256]{2,1,0:T(8,128)S(1)}, f32[1,160,256]{2,1,0:T(8,128)S(1)}, u32[]{:S(2)}, u32[]{:S(2)}) collective-permute-start(f32[1,160,256]{2,1,0:T(8,128)S(1)} %get-tuple-element.58), channel_id=1, source_target_pairs={{0,4},{4,0},{8,12},{12,8},{1,5},{5,1},{9,13},{13,9},{2,6},{6,2},{1... | collective-permute-start | bytes 491528 | tf_op jit(solution)/shard_map/ppermute | solution.py:44
  89.6 1.7 %collective-permute-start.24 = (f32[2,160,256]{2,1,0:T(8,128)S(1)}, f32[2,160,256]{2,1,0:T(8,128)S(1)}, u32[]{:S(2)}, u32[]{:S(2)}) collective-permute-start(f32[2,160,256]{2,1,0:T(8,128)S(1)} %get-tuple-element.66), channel_id=1, source_target_pairs={{0,16},{16,0},{1,17},{17,1},{2,18},{18,2},{3,19},{19,3},{4,20},{20... | collective-permute-start | bytes 983048 | tf_op jit(solution)/shard_map/ppermute | solution.py:44
  89.7 2.1 %collective-permute-start.25 = (f32[2,160,256]{2,1,0:T(8,128)S(1)}, f32[2,160,256]{2,1,0:T(8,128)S(1)}, u32[]{:S(2)}, u32[]{:S(2)}) collective-permute-start(f32[2,160,256]{2,1,0:T(8,128)S(1)} %get-tuple-element.67), channel_id=1, source_target_pairs={{0,16},{16,0},{1,17},{17,1},{2,18},{18,2},{3,19},{19,3},{4,20},{20... | collective-permute-start | bytes 983048 | tf_op jit(solution)/shard_map/ppermute | solution.py:44
  91.9 9.8 %collective-permute-start.27 = (f32[1,160,256]{2,1,0:T(8,128)S(1)}, f32[1,160,256]{2,1,0:T(8,128)S(1)}, u32[]{:S(2)}, u32[]{:S(2)}) collective-permute-start(f32[1,160,256]{2,1,0:T(8,128)S(1)} %get-tuple-element.70), channel_id=1, source_target_pairs={{0,8},{4,12},{8,0},{12,4},{1,9},{5,13},{9,1},{13,5},{2,10},{6,14},... | collective-permute-start | bytes 491528 | tf_op jit(solution)/shard_map/ppermute | solution.py:44
  93.5 8.2 %collective-permute-start.28 = (f32[1,160,256]{2,1,0:T(8,128)S(1)}, f32[1,160,256]{2,1,0:T(8,128)S(1)}, u32[]{:S(2)}, u32[]{:S(2)}) collective-permute-start(f32[1,160,256]{2,1,0:T(8,128)S(1)} %get-tuple-element.71), channel_id=1, source_target_pairs={{0,12},{4,8},{8,4},{12,0},{1,13},{5,9},{9,5},{13,1},{2,14},{6,10},... | collective-permute-start | bytes 491528 | tf_op jit(solution)/shard_map/ppermute | solution.py:44
  94.9 8.0 %collective-permute-start.26 = (f32[1,160,256]{2,1,0:T(8,128)S(1)}, f32[1,160,256]{2,1,0:T(8,128)S(1)}, u32[]{:S(2)}, u32[]{:S(2)}) collective-permute-start(f32[1,160,256]{2,1,0:T(8,128)S(1)} %get-tuple-element.69), channel_id=1, source_target_pairs={{0,4},{4,0},{8,12},{12,8},{1,5},{5,1},{9,13},{13,9},{2,6},{6,2},{1... | collective-permute-start | bytes 491528 | tf_op jit(solution)/shard_map/ppermute | solution.py:44
  103.0 10.6 %collective-permute-start.30 = (f32[3,32,256]{2,1,0:T(8,128)S(1)}, f32[3,32,256]{2,1,0:T(8,128)S(1)}, u32[]{:S(2)}, u32[]{:S(2)}) collective-permute-start(f32[3,32,256]{2,1,0:T(8,128)S(1)} %cut.1), channel_id=1, source_target_pairs={{0,2},{1,3},{2,0},{3,1},{4,6},{5,7},{6,4},{7,5},{8,10},{9,11},{10,... | collective-permute-start | bytes 294920 | tf_op jit(solution)/shard_map/ppermute | solution.py:44
  106.5 7.3 %collective-permute-start.31 = (f32[3,32,256]{2,1,0:T(8,128)S(1)}, f32[3,32,256]{2,1,0:T(8,128)S(1)}, u32[]{:S(2)}, u32[]{:S(2)}) collective-permute-start(f32[3,32,256]{2,1,0:T(8,128)S(1)} %cut.1), channel_id=1, source_target_pairs={{0,3},{1,2},{2,1},{3,0},{4,7},{5,6},{6,5},{7,4},{8,11},{9,10},{10,... | collective-permute-start | bytes 294920 | tf_op jit(solution)/shard_map/ppermute | solution.py:44
  108.0 6.5 %collective-permute-start.29 = (f32[3,32,256]{2,1,0:T(8,128)S(1)}, f32[3,32,256]{2,1,0:T(8,128)S(1)}, u32[]{:S(2)}, u32[]{:S(2)}) collective-permute-start(f32[3,32,256]{2,1,0:T(8,128)S(1)} %cut.1), channel_id=1, source_target_pairs={{0,1},{1,0},{2,3},{3,2},{4,5},{5,4},{6,7},{7,6},{8,9},{9,8},{10,11... | collective-permute-start | bytes 294920 | tf_op jit(solution)/shard_map/ppermute | solution.py:44
  114.5 5.6 %collective-permute-start.34 = (f32[3,32,256]{2,1,0:T(8,128)S(1)}, f32[3,32,256]{2,1,0:T(8,128)S(1)}, u32[]{:S(2)}, u32[]{:S(2)}) collective-permute-start(f32[3,32,256]{2,1,0:T(8,128)S(1)} %add_add_fusion.3), channel_id=1, source_target_pairs={{0,12},{4,8},{8,4},{12,0},{1,13},{5,9},{9,5},{13,1},{2,14},{6,10},... | collective-permute-start | bytes 294920 | tf_op jit(solution)/shard_map/ppermute | solution.py:44
  117.0 4.6 %collective-permute-start.33 = (f32[3,32,256]{2,1,0:T(8,128)S(1)}, f32[3,32,256]{2,1,0:T(8,128)S(1)}, u32[]{:S(2)}, u32[]{:S(2)}) collective-permute-start(f32[3,32,256]{2,1,0:T(8,128)S(1)} %add_add_fusion.3), channel_id=1, source_target_pairs={{0,8},{4,12},{8,0},{12,4},{1,9},{5,13},{9,1},{13,5},{2,10},{6,14},... | collective-permute-start | bytes 294920 | tf_op jit(solution)/shard_map/ppermute | solution.py:44
  117.5 4.6 %collective-permute-start.32 = (f32[3,32,256]{2,1,0:T(8,128)S(1)}, f32[3,32,256]{2,1,0:T(8,128)S(1)}, u32[]{:S(2)}, u32[]{:S(2)}) collective-permute-start(f32[3,32,256]{2,1,0:T(8,128)S(1)} %add_add_fusion.3), channel_id=1, source_target_pairs={{0,4},{4,0},{8,12},{12,8},{1,5},{5,1},{9,13},{13,9},{2,6},{6,2},{1... | collective-permute-start | bytes 294920 | tf_op jit(solution)/shard_map/ppermute | solution.py:44
  122.3 1.8 %collective-permute-start.35 = (f32[4,3,32,256]{3,2,0,1:T(8,128)S(1)}, f32[4,3,32,256]{3,2,0,1:T(8,128)S(1)}, u32[]{:S(2)}, u32[]{:S(2)}) collective-permute-start(f32[4,3,32,256]{3,2,0,1:T(8,128)S(1)} %copy.10), channel_id=1, source_target_pairs={{0,16},{16,0},{1,17},{17,1},{2,18},{18,2},{3,19},{19,3},{4,20},{20... | collective-permute-start | bytes 1179656 | tf_op jit(solution)/shard_map/ppermute | solution.py:44
